TPU v7x, 32 devices: a whole 2x2x4 slice. The times are simulated.
32 devices in a mesh: group: 2 (over y), shard: 16 (over z, x, core).
Axes of the slice: x: 2, y: 2, z: 4, core: 2. Of those that a mesh axis runs over, the one named last changes fastest.
Arguments:
- activations: bfloat16 [2, 128, 64, 1024], P('group', 'shard'), may hold values from -7 to 7
- out_grad: bfloat16 [2, 128, 64, 1024], P('group', None, 'shard'), may hold values from -1.5 to 1.5
- embedding: bfloat16 [512, 1024], replicated, may hold values from -6 to 6
- counts: int32 [2, 2], P('group'), may hold values from 0 to 64, as said below
- offsets: int32 [2, 2], P('group'), may hold values from 0 to 2, as said below
- layout: int32 [2, 64], P('group'), may hold values from 0 to 511
Outputs:
- input_grad: bfloat16 [2, 128, 64, 1024], P('group', 'shard')
- embedding_grad: float32 [512, 1024], P('group')
Inputs may be any that keep to these rules, and one draw needn't show every extreme that they name: `counts`: A used session slot holds 19 to 256 electrodes; slots after the used ones hold 0. `offsets`: used session slots come first; the first starts at block 0 and each next one where the previous ends, a session taking ceil(count / 32) blocks, all sessions together exactly 2 blocks; unused slots hold 2.
All inputs are finite; a program needn't handle non-finite values.
Results may differ from a plain program's by a relative error of at most 0.012.
The roundings to bfloat16 on the way count: a program that leaves them out, or rounds other values in their place, can miss the bound.
Values may be sent and summed in bfloat16 or wider, within the bound.
No kernel may reach another device: no remote copies, remote signals or barrier semaphores. Data moves between devices by JAX's collectives and lax.ppermute only.
A program may use at most 64 MiB of HBM per device.

v0:
```python
import functools
import math

import jax
import jax.numpy as jnp
from jax import lax
from jax.experimental import pallas as pl
from jax.experimental.pallas import tpu as pltpu
from jax.sharding import PartitionSpec as P

HEADS = 16
BLOCK = 32
LANES = 128
MASKED = -1e30
SUBLANES = 8
STEP = 512
PIECES = 4
PLANE = 4
SPATIAL_GROUP = 32
TEMPORAL_GROUP = 8


def dot(left, right, over):
    return lax.dot_general(
        left, right, (((over[0],), (over[1],)), ((), ())), preferred_element_type=jnp.float32
    )


def head_masks(width, scale):
    lane = lax.broadcasted_iota(jnp.int32, (1, LANES), 1)
    first = jnp.where(lane < width, scale, 0.0).astype(jnp.bfloat16)
    second = jnp.where(lane < width, 0.0, scale).astype(jnp.bfloat16)
    return first, second


def head_rows(pair, masks):
    return jnp.concatenate([pair * masks[0], pair * masks[1]], axis=0)


def head_columns(rows, width):
    count = rows.shape[0] // 2
    lane = lax.broadcasted_iota(jnp.int32, (count, rows.shape[1]), 1)
    return jnp.where(lane < width, rows[:count], rows[count:])


def each(function, *lists):
    return [function(*items) for items in zip(*lists)]


def weights_by_key(scores):
    tops = each(lambda s: jnp.max(s, axis=0, keepdims=True), scores)
    exponents = each(lambda s, t: jnp.exp(s - t), scores, tops)
    shares = each(lambda e: 1.0 / jnp.sum(e, axis=0, keepdims=True), exponents)
    return each(lambda e, r: (e * r).astype(jnp.bfloat16), exponents, shares)


def by_query(shares, values, width):
    if 2 * values[0].shape[0] != LANES or len(values) % 2:
        return each(lambda s, v: head_columns(dot(s, v, (0, 0)), width), shares, values)
    results = []
    for first in range(0, len(values), 2):
        turned = jnp.transpose(jnp.concatenate(shares[first : first + 2], axis=0))
        one, other = values[first : first + 2]
        zero = jnp.zeros_like(one)
        apart = jnp.concatenate(
            [jnp.concatenate([one, zero], axis=1), jnp.concatenate([zero, other], axis=1)], axis=0
        )
        both = dot(turned, apart, (1, 0))
        results += [head_columns(both[:, :LANES], width), head_columns(both[:, LANES:], width)]
    return results


def back(values, scaled, cotangents, weights, grad_weights, heads_grads, width):
    wide = each(lambda w: w.astype(jnp.float32), weights)
    deltas = each(lambda w, g: jnp.sum(w * g, axis=0, keepdims=True), wide, grad_weights)
    grad_scores = each(
        lambda w, g, d: (w * (g - d)).astype(jnp.bfloat16), wide, grad_weights, deltas
    )
    length = values[0].shape[0]
    whole = length % LANES == 0
    both_ways = grad_scores
    if whole:
        both_ways = each(
            lambda g: jnp.concatenate(
                [
                    g[:, start : start + length] + jnp.transpose(g[:, start : start + length])
                    for start in (0, length)
                ],
                axis=1,
            ),
            grad_scores,
        )
    grads = each(
        lambda c, w, g, hg, hv: c.astype(jnp.float32)
        + dot(jnp.concatenate([w, g], axis=1), jnp.concatenate([hg, hv], axis=0), (1, 0)),
        cotangents,
        weights,
        both_ways,
        heads_grads,
        scaled,
    )
    if whole:
        return grads
    score_scale = 0.5 / math.sqrt(width)
    rest = by_query(grad_scores, values, width)
    return each(lambda g, r: g + score_scale * r, grads, rest)


def pair_bias(counts, offsets, slots):
    def sessions(slot):
        block = slot // BLOCK
        session = jnp.full(slot.shape, -1, jnp.int32)
        for j in range(offsets.shape[1]):
            session = session + (offsets[0, j] <= block).astype(jnp.int32)
        return session

    key_slot = lax.broadcasted_iota(jnp.int32, (slots, 2 * slots), 0)
    query_slot = lax.broadcasted_iota(jnp.int32, (slots, 2 * slots), 1) % slots
    key_session = sessions(key_slot)
    first = jnp.zeros_like(key_slot)
    live = jnp.zeros_like(key_slot)
    for j in range(offsets.shape[1]):
        chosen = key_session == j
        first = jnp.where(chosen, offsets[0, j] * BLOCK, first)
        live = jnp.where(chosen, counts[0, j], live)
    allowed = (key_session == sessions(query_slot)) & (key_slot - first < live)
    return jnp.where(allowed, 0.0, MASKED)


def pair_columns(pair):
    return pl.ds(pair * LANES, LANES)


def in_groups(pairs, rows, size):
    items = [(pair, row) for pair in range(pairs) for row in range(rows)]
    return [items[start : start + size] for start in range(0, len(items), size)]


def of_patch(patch, slots, patches):
    return pl.ds(patch, slots, stride=patches)


def attention(width, tokens, rows, bias, group):
    score_masks = head_masks(width, 0.5 / math.sqrt(width))
    values = [
        (
            tokens[p, :, pair_columns(pair)].astype(jnp.float32)
            + rows[:, pair * LANES : (pair + 1) * LANES]
        ).astype(jnp.bfloat16)
        for pair, p in group
    ]
    scores = each(lambda v: dot(v, head_rows(v, score_masks), (1, 1)) + bias[...], values)
    return values, weights_by_key(scores)


def spatial_kernel(
    width, counts, offsets, layout, embedding, tokens, rows, mixed, spread, bias, by_electrode
):
    patches, slots, model = tokens.shape
    templates = embedding.shape[0]
    pairs = model // LANES

    @pl.when(pl.program_id(0) == 0)
    def _():
        bias[...] = pair_bias(counts, offsets, slots)
        chosen = lax.broadcasted_iota(jnp.int32, (templates, slots), 0) == layout[...]
        spread[...] = jnp.transpose(chosen.astype(jnp.float32)).astype(jnp.bfloat16)

    chosen_rows = dot(spread[...], embedding[...], (1, 0))
    rows[...] = chosen_rows.astype(jnp.bfloat16)
    for group in in_groups(pairs, patches, SPATIAL_GROUP):
        values, shares = attention(width, tokens, chosen_rows, bias, group)
        attended = by_query(shares, values, width)
        for (pair, p), value, result in zip(group, values, attended):
            by_electrode[pair, of_patch(p, slots, patches), :] = value.astype(jnp.float32) + result
    for pair in range(pairs):
        mixed[:, pair_columns(pair)] = by_electrode[pair].astype(jnp.bfloat16)


def weights_kernel(width, counts, offsets, rows, tokens, embedded, weights, made, bias):
    made[...] = jnp.zeros_like(made)
    patches, slots, model = tokens.shape

    @pl.when(pl.program_id(0) == 0)
    def _():
        bias[...] = pair_bias(counts, offsets, slots)

    added = rows[...].astype(jnp.float32)
    for group in in_groups(model // LANES, patches, SPATIAL_GROUP):
        values, shares = attention(width, tokens, added, bias, group)
        for (pair, p), value, share in zip(group, values, shares):
            embedded[p, :, pair_columns(pair)] = value
            weights[p, pair] = share


def patches_first(local):
    return local % SUBLANES != 0


def electrode_rows(electrode, electrodes, parts, local):
    start, step = electrode * local, electrodes * local
    if patches_first(local):
        return [pl.ds(start + p, parts, stride=step) for p in range(local)]
    return [pl.ds(start + part * step, local) for part in range(parts)]


def temporal_kernel(width, parts, mixed, out_grad, *refs):
    mixed_grad, received, returned = refs[-3:]
    electrodes, patches, model = out_grad.shape
    local = patches // parts
    pairs = model // LANES
    score_masks = head_masks(width, 0.5 / math.sqrt(width))
    ones = head_masks(width, 1.0)
    for pair in range(pairs):
        received[pair] = mixed[:, pair_columns(pair)].astype(jnp.float32)
    for group in in_groups(pairs, electrodes, TEMPORAL_GROUP):
        places = [electrode_rows(e, electrodes, parts, local) for _, e in group]
        values = each(
            lambda item, place: jnp.concatenate(
                [received[item[0], rows, :] for rows in place], axis=0
            ).astype(jnp.bfloat16),
            group,
            places,
        )
        cotangents = [out_grad[e, :, pair_columns(pair)] for pair, e in group]
        scaled = each(lambda v: head_rows(v, score_masks), values)
        scores = each(lambda v, s: dot(v, s, (1, 1)), values, scaled)
        heads_grads = each(lambda g: head_rows(g, ones), cotangents)
        grad_weights = each(lambda v, g: dot(v, g, (1, 1)), values, heads_grads)
        shares = weights_by_key(scores)
        grads = back(values, scaled, cotangents, shares, grad_weights, heads_grads, width)
        for (pair, _), place, grad in zip(group, places, grads):
            start = 0
            for rows in place:
                returned[pair, rows, :] = grad[start : start + rows.size]
                start += rows.size
    for pair in range(pairs):
        mixed_grad[:, pair_columns(pair)] = returned[pair].astype(jnp.bfloat16)


def half_rows(bit, away, count):
    here = lax.bitwise_and(lax.shift_right_logical(lax.axis_index("shard"), bit), 1)
    return pl.ds(pl.multiple_of(lax.bitwise_xor(here, away) * count, count), count)


def spatial_back_kernel(width, embedded, weights, mixed_grad, input_grad, *refs):
    electrode_grads, (sums, received) = refs[:-2], refs[-2:]
    patches, slots, model = embedded.shape
    pairs = model // LANES
    score_masks = head_masks(width, 0.5 / math.sqrt(width))
    ones = head_masks(width, 1.0)
    totals = [jnp.zeros((slots, LANES), jnp.float32) for _ in range(pairs)]
    for pair in range(pairs):
        received[pair] = mixed_grad[:, pair_columns(pair)].astype(jnp.float32)
    for group in in_groups(pairs, patches, SPATIAL_GROUP):
        cotangents = [
            received[pair, of_patch(p, slots, patches), :].astype(jnp.bfloat16)
            for pair, p in group
        ]
        values = [embedded[p, :, pair_columns(pair)] for pair, p in group]
        shares = [weights[p, pair] for pair, p in group]
        scaled = each(lambda v: head_rows(v, score_masks), values)
        heads_grads = each(lambda g: head_rows(g, ones), cotangents)
        grad_weights = each(lambda v, g: dot(v, g, (1, 1)), values, heads_grads)
        grads = back(values, scaled, cotangents, shares, grad_weights, heads_grads, width)
        for (pair, p), grad in zip(group, grads):
            input_grad[p, :, pair_columns(pair)] = grad.astype(jnp.bfloat16)
            totals[pair] = totals[pair] + grad
    for pair in range(pairs):
        sums[pair] = totals[pair]
        for away, block in enumerate(electrode_grads):
            rows = sums[pair, half_rows(0, away, block.shape[0]), :]
            block[:, pair_columns(pair)] = rows.astype(jnp.bfloat16)


def add(one, other):
    return (one.astype(jnp.float32) + other.astype(jnp.float32)).astype(jnp.bfloat16)


def core_sum_kernel(own, arrived, total):
    total[...] = add(own[...], arrived[...])


def cross_sum_kernel(*refs):
    totals = refs[-1]
    for away in range(totals.shape[0]):
        totals[away] = add(refs[2 * away][...], refs[2 * away + 1][...])


def far_sum_kernel(*refs):
    parts, (total, ordered) = refs[:-2], refs[-2:]
    place = lax.div(lax.axis_index("shard"), PLANE)
    for away, part in enumerate(parts):
        ordered[lax.bitwise_xor(place, away)] = part[...].astype(jnp.float32)
    result = ordered[0]
    for index in range(1, len(parts)):
        result = result + ordered[index]
    total[...] = result.astype(jnp.bfloat16)


def join_kernel(bit, own, arrived, joined):
    for away, block in enumerate((own, arrived)):
        joined[:, half_rows(bit, away, block.shape[1]), :] = block[...]


def table_kernel(groups, *refs):
    layouts, blocks, (table, sources, pieces, sems) = refs[:groups], refs[groups:-4], refs[-4:]
    owner = lax.axis_index("group")
    count, rows, _ = pieces.shape
    slots = sources.shape[1]
    join_kernel(0, *blocks, sources)
    copies = []
    for piece in range(count):
        first = owner * (count * rows) + piece * rows
        template = lax.broadcasted_iota(jnp.int32, (rows, slots), 0) + first
        total = jnp.zeros(pieces.shape[1:], jnp.float32)
        for away in range(groups):
            spread = (template == layouts[away][...]).astype(jnp.float32).astype(jnp.bfloat16)
            total = total + dot(spread, sources[away], (1, 0))
        pieces[piece] = total
        copy = pltpu.make_async_copy(
            pieces.at[piece], table.at[pl.ds(piece * rows, rows)], sems.at[piece]
        )
        copy.start()
        copies.append(copy)
    for copy in copies:
        copy.wait()


VMEM = pl.BlockSpec(memory_space=pltpu.VMEM)
SMEM = pl.BlockSpec(memory_space=pltpu.SMEM)
HBM = pl.BlockSpec(memory_space=pltpu.HBM)
PARAMS = pltpu.CompilerParams(vmem_limit_bytes=32 * 1024 * 1024)
STREAMED = pltpu.CompilerParams(vmem_limit_bytes=56 * 1024 * 1024)


def body(activations, out_grad, embedding, counts, offsets, layout):
    tokens = activations[0]
    local, slots, model = tokens.shape
    groups = lax.axis_size("group")
    parts = lax.axis_size("shard")
    patches = local * parts
    own = slots // parts
    width = model // HEADS
    templates = embedding.shape[0]
    pairs = STEP // LANES
    steps = model // STEP

    layouts = [layout] + [
        lax.ppermute(layout, "group", [(i, (i + away) % groups) for i in range(groups)])
        for away in range(1, groups)
    ]
    order = (2, 1, 0, 3) if patches_first(local) else (2, 0, 1, 3)
    cotangent = jnp.transpose(out_grad[0].reshape(parts, local, own, model), order)
    cotangent = cotangent.reshape(own, patches, model)

    flat = pl.BlockSpec((slots * local, STEP), lambda step: (0, step))
    planes = pl.BlockSpec((local, slots, STEP), lambda step: (0, 0, step))
    squares = pl.BlockSpec((local, pairs, slots, 2 * slots), lambda step: (0, step, 0, 0))
    flat_shape = jax.ShapeDtypeStruct((slots * local, model), jnp.bfloat16)
    plane_shape = jax.ShapeDtypeStruct(tokens.shape, jnp.bfloat16)
    flat_scratch = pltpu.VMEM((pairs, slots * local, LANES), jnp.float32)

    strip = pl.BlockSpec((slots, STEP), lambda step: (0, step))
    rows, mixed = pl.pallas_call(
        functools.partial(spatial_kernel, width),
        grid=(steps,),
        out_shape=(jax.ShapeDtypeStruct((slots, model), jnp.bfloat16), flat_shape),
        in_specs=[SMEM, SMEM, VMEM, pl.BlockSpec((templates, STEP), lambda step: (0, step)), planes],
        out_specs=(strip, flat),
        scratch_shapes=[
            pltpu.VMEM((slots, templates), jnp.bfloat16),
            pltpu.VMEM((slots, 2 * slots), jnp.float32),
            flat_scratch,
        ],
        compiler_params=STREAMED,
        name="spatial",
    )(counts, offsets, layout, embedding, tokens)
    embedded, weights, made = pl.pallas_call(
        functools.partial(weights_kernel, width),
        grid=(steps,),
        out_shape=(
            plane_shape,
            jax.ShapeDtypeStruct((local, model // LANES, slots, 2 * slots), jnp.bfloat16),
            jax.ShapeDtypeStruct((SUBLANES, LANES), jnp.float32),
        ),
        in_specs=[SMEM, SMEM, strip, planes],
        out_specs=(planes, squares, pl.BlockSpec((SUBLANES, LANES), lambda step: (0, 0))),
        scratch_shapes=[pltpu.VMEM((slots, 2 * slots), jnp.float32)],
        compiler_params=STREAMED,
        cost_estimate=pl.CostEstimate(
            flops=4 * local * slots * slots * model, bytes_accessed=6 * tokens.size, transcendentals=0
        ),
        name="weights",
    )(counts, offsets, rows, tokens)

    gathered = lax.all_to_all(mixed, "shard", split_axis=0, concat_axis=0, tiled=True)
    mixed_grad = pl.pallas_call(
        functools.partial(temporal_kernel, width, parts),
        grid=(steps,),
        out_shape=flat_shape,
        in_specs=[flat, pl.BlockSpec((own, patches, STEP), lambda step: (0, 0, step))]
        + [pl.BlockSpec(memory_space=pl.ANY)] * groups,
        out_specs=flat,
        scratch_shapes=[flat_scratch, flat_scratch],
        compiler_params=PARAMS,
        name="temporal",
    )(gathered, cotangent, made, *layouts[1:])

    returned = lax.all_to_all(mixed_grad, "shard", split_axis=0, concat_axis=0, tiled=True)
    half = slots // 2
    input_grad, own_half, other_half = pl.pallas_call(
        functools.partial(spatial_back_kernel, width),
        grid=(steps,),
        out_shape=(plane_shape,) + (jax.ShapeDtypeStruct((half, model), jnp.bfloat16),) * 2,
        in_specs=[planes, squares, flat],
        out_specs=(planes,) + (pl.BlockSpec((half, STEP), lambda step: (0, step)),) * 2,
        scratch_shapes=[pltpu.VMEM((pairs, slots, LANES), jnp.float32), flat_scratch],
        compiler_params=PARAMS,
        name="spatial_back",
    )(embedded, weights, returned)

    far_count = parts // PLANE
    assert parts == far_count * PLANE and parts & (parts - 1) == 0

    def to_partner(array, group_away, shard_away):
        if group_away == 0 and shard_away == 0:
            return array
        pairs_of_devices = [
            (g * parts + i, (g + group_away) % groups * parts + (i ^ shard_away))
            for g in range(groups)
            for i in range(parts)
        ]
        return lax.ppermute(array, ("group", "shard"), pairs_of_devices)

    def summed(kernel, shape, operands, scratch=()):
        return pl.pallas_call(
            kernel,
            out_shape=jax.ShapeDtypeStruct(shape, jnp.bfloat16),
            in_specs=[VMEM] * len(operands),
            out_specs=VMEM,
            scratch_shapes=list(scratch),
            compiler_params=PARAMS,
            name="sums",
        )(*operands)

    halved = summed(core_sum_kernel, (half, model), (own_half, to_partner(other_half, 0, 1)))
    total = summed(
        far_sum_kernel,
        (half, model),
        [to_partner(halved, 0, far * PLANE) for far in range(far_count)],
        [pltpu.VMEM((far_count, half, model), jnp.float32)],
    )
    crossed = [
        to_partner(total, away, side) for away in reversed(range(groups)) for side in (2, 0)
    ]
    totals = summed(cross_sum_kernel, (groups, half, model), crossed[::-1])
    table_rows = templates // groups
    table_grad = pl.pallas_call(
        functools.partial(table_kernel, groups),
        out_shape=jax.ShapeDtypeStruct((table_rows, model), jnp.float32),
        in_specs=[VMEM] * (groups + 2),
        out_specs=HBM,
        scratch_shapes=[
            pltpu.VMEM((groups, slots, model), jnp.bfloat16),
            pltpu.VMEM((PIECES, table_rows // PIECES, model), jnp.float32),
            pltpu.SemaphoreType.DMA((PIECES,)),
        ],
        compiler_params=PARAMS,
        name="table",
    )(*layouts, totals, to_partner(totals, 0, 1))
    return (input_grad[None], table_grad)


def solution(mesh):
    placed = (
        P("group", "shard", None, None),
        P("group", None, "shard", None),
        P(),
        P("group", None),
        P("group", None),
        P("group", None),
    )
    return jax.shard_map(
        body,
        mesh=mesh,
        in_specs=placed,
        out_specs=(P("group", "shard", None, None), P("group", None)),
        check_vma=False,
    )
```

profile of v0, /device:TPU:0, one launch (start us, length us, event | category | flops | bytes accessed | tf_op | source)
XLA Modules:
  0.0 97.9 jit_solution(14769560658915299456)
XLA Ops:
  0.6 5.1 %spatial.1 = (bf16[64,1024]{1,0:T(8,128)(2,1)}, bf16[512,1024]{1,0:T(8,128)(2,1)}) custom-call(s32[1,2]{1,0:T(1,128)} %counts.3, s32[1,2]{1,0:T(1,128)} %offsets.3, s32[1,64]{1,0:T(1,128)} %refs_0_.1, bf16[512,1024]{1,0:T(8,128)(2,1)} %embedding.1, bf16[8,64,1024]{2,1,0:T(8,128)(2,1)} %bitcast.16), custom_call_target="tpu_custom_call" | custom-call | tf_op jit(solution)/shard_map/spatial/pallas_call | solution.py:365
  5.7 7.5 %all-to-all-start = ((bf16[16,32,1024]{2,1,0:T(8,128)(2,1)}), bf16[16,32,1024]{2,1,0:T(8,128)(2,1)S(1)}, u32[]{:S(2)}, u32[]{:S(2)}) async-start(bf16[16,32,1024]{2,1,0:T(8,128)(2,1)} %bitcast.19), calls=%async_computation | async-start | bytes 2097152 | tf_op jit(solution)/shard_map/all_to_all | solution.py:397
  13.2 1.6 %collective-permute-start = (s32[1,64]{1,0:T(1,128)S(1)}, s32[1,64]{1,0:T(1,128)S(1)}, u32[]{:S(2)}, u32[]{:S(2)}) collective-permute-start(s32[1,64]{1,0:T(1,128)S(1)} %copy-done.3), channel_id=1, source_target_pairs={{0,16},{16,0},{1,17},{17,1},{2,18},{18,2},{3,19},{19,3},{4,20},{20... | collective-permute-start | bytes 776 | tf_op jit(solution)/shard_map/ppermute | solution.py:350
  14.8 3.7 %weights.1 = (bf16[8,64,1024]{2,1,0:T(8,128)(2,1)}, bf16[8,8,64,128]{3,2,1,0:T(8,128)(2,1)}, f32[8,128]{1,0:T(8,128)}) custom-call(s32[1,2]{1,0:T(1,128)} %counts.3, s32[1,2]{1,0:T(1,128)} %offsets.3, bf16[64,1024]{1,0:T(8,128)(2,1)} %get-tuple-element.10.rows, bf16[8,64,1024]{2,1,0:T(8,128)(2,1)} %bitcast.17), custom_call_target="tpu_custom_call" | custom-call | flops 134217728 | bytes 3145728 | tf_op jit(solution)/shard_map/weights/pallas_call | solution.py:379
  18.5 0.3 copy.10
  18.9 17.3 %all-to-all-done = bf16[16,32,1024]{2,1,0:T(8,128)(2,1)S(1)} async-done(((bf16[16,32,1024]{2,1,0:T(8,128)(2,1)}), bf16[16,32,1024]{2,1,0:T(8,128)(2,1)S(1)}, u32[]{:S(2)}, u32[]{:S(2)}) %all-to-all-start) | async-done | bytes 1048608 | tf_op jit(solution)/shard_map/all_to_all | solution.py:397
  36.1 4.1 %temporal.1 = bf16[512,1024]{1,0:T(8,128)(2,1)S(1)} custom-call(bf16[512,1024]{1,0:T(8,128)(2,1)S(1)} %bitcast.13, bf16[4,128,1024]{2,1,0:T(8,128)(2,1)S(1)} %bitcast.14, f32[8,128]{1,0:T(8,128)S(1)} %copy-done.2, s32[1,64]{1,0:T(1,128)S(1)} %collective-permute-done.refs_1_), custom_call_target="tpu_custom_call" | custom-call | tf_op jit(solution)/shard_map/temporal/pallas_call | solution.py:398
  40.3 31.6 %all_to_all.22 = bf16[16,32,1024]{2,1,0:T(8,128)(2,1)S(1)} all-to-all(bf16[16,32,1024]{2,1,0:T(8,128)(2,1)S(1)} %bitcast.15), channel_id=1, replica_groups=mesh['group'=2,'shard'=16] {'shard'}, dimensions={0} | all-to-all | bytes 2097152 | tf_op jit(solution)/shard_map/all_to_all | solution.py:410
  71.9 4.0 %spatial_back.1 = (bf16[8,64,1024]{2,1,0:T(8,128)(2,1)}, bf16[32,1024]{1,0:T(8,128)(2,1)S(1)}, bf16[32,1024]{1,0:T(8,128)(2,1)S(1)}) custom-call(bf16[8,64,1024]{2,1,0:T(8,128)(2,1)S(1)} %copy-done, bf16[8,8,64,128]{3,2,1,0:T(8,128)(2,1)S(1)} %copy-done.1, bf16[512,1024]{1,0:T(8,128)(2,1)S(1)} %bitcast.12), custom_call_target="tpu_custom_call" | custom-call | tf_op jit(solution)/shard_map/spatial_back/pallas_call | solution.py:412
  75.9 0.8 collective-permute-start.1
  76.7 0.9 collective-permute-done.1.arrived
  77.6 1.9 %collective-permute-start.2 = (bf16[32,1024]{1,0:T(8,128)(2,1)S(1)}, bf16[32,1024]{1,0:T(8,128)(2,1)S(1)}, u32[]{:S(2)}, u32[]{:S(2)}) collective-permute-start(bf16[32,1024]{1,0:T(8,128)(2,1)S(1)} %sums.3.refs_0_), channel_id=1, source_target_pairs={{0,4},{1,5},{2,6},{3,7},{4,0},{5,1},{6,2},{7,3},{8,12},{9,13},{10,... | collective-permute-start | bytes 196616 | tf_op jit(solution)/shard_map/ppermute | solution.py:434
  79.5 0.9 collective-permute-start.3
  80.4 1.6 %collective-permute-start.4 = (bf16[32,1024]{1,0:T(8,128)(2,1)S(1)}, bf16[32,1024]{1,0:T(8,128)(2,1)S(1)}, u32[]{:S(2)}, u32[]{:S(2)}) collective-permute-start(bf16[32,1024]{1,0:T(8,128)(2,1)S(1)} %sums.3.refs_0_), channel_id=1, source_target_pairs={{0,12},{1,13},{2,14},{3,15},{4,8},{5,9},{6,10},{7,11},{8,4},{9,5},... | collective-permute-start | bytes 196616 | tf_op jit(solution)/shard_map/ppermute | solution.py:434
  82.1 5.6 %collective-permute-done.3.refs_2_ = bf16[32,1024]{1,0:T(8,128)(2,1)S(1)} collective-permute-done((bf16[32,1024]{1,0:T(8,128)(2,1)S(1)}, bf16[32,1024]{1,0:T(8,128)(2,1)S(1)}, u32[]{:S(2)}, u32[]{:S(2)}) %collective-permute-start.3) | collective-permute-done | bytes 65568 | tf_op jit(solution)/shard_map/ppermute | solution.py:434
  87.8 0.7 collective-permute-start.5
  88.5 1.5 %collective-permute-start.6 = (bf16[32,1024]{1,0:T(8,128)(2,1)S(1)}, bf16[32,1024]{1,0:T(8,128)(2,1)S(1)}, u32[]{:S(2)}, u32[]{:S(2)}) collective-permute-start(bf16[32,1024]{1,0:T(8,128)(2,1)S(1)} %sums.4.refs_0_), channel_id=1, source_target_pairs={{0,16},{1,17},{2,18},{3,19},{4,20},{5,21},{6,22},{7,23},{8,24},{9,... | collective-permute-start | bytes 196616 | tf_op jit(solution)/shard_map/ppermute | solution.py:434
  90.0 1.4 %collective-permute-start.7 = (bf16[32,1024]{1,0:T(8,128)(2,1)S(1)}, bf16[32,1024]{1,0:T(8,128)(2,1)S(1)}, u32[]{:S(2)}, u32[]{:S(2)}) collective-permute-start(bf16[32,1024]{1,0:T(8,128)(2,1)S(1)} %sums.4.refs_0_), channel_id=1, source_target_pairs={{0,18},{1,19},{2,16},{3,17},{4,22},{5,23},{6,20},{7,21},{8,26},{9,... | collective-permute-start | bytes 196616 | tf_op jit(solution)/shard_map/ppermute | solution.py:434
  91.4 1.1 %collective-permute-done.5.refs_1_ = bf16[32,1024]{1,0:T(8,128)(2,1)S(1)} collective-permute-done((bf16[32,1024]{1,0:T(8,128)(2,1)S(1)}, bf16[32,1024]{1,0:T(8,128)(2,1)S(1)}, u32[]{:S(2)}, u32[]{:S(2)}) %collective-permute-start.5) | collective-permute-done | bytes 65568 | tf_op jit(solution)/shard_map/ppermute | solution.py:434
  92.4 1.0 collective-permute-done.6.refs_2_
  93.4 1.8 %collective-permute-done.7.refs_3_ = bf16[32,1024]{1,0:T(8,128)(2,1)S(1)} collective-permute-done((bf16[32,1024]{1,0:T(8,128)(2,1)S(1)}, bf16[32,1024]{1,0:T(8,128)(2,1)S(1)}, u32[]{:S(2)}, u32[]{:S(2)}) %collective-permute-start.7) | collective-permute-done | bytes 65568 | tf_op jit(solution)/shard_map/ppermute | solution.py:434
  95.2 0.1 collective-permute-start.8
  95.3 1.3 %collective-permute-done.8.refs_3_ = bf16[2,32,1024]{2,1,0:T(8,128)(2,1)S(1)} collective-permute-done((bf16[2,32,1024]{2,1,0:T(8,128)(2,1)S(1)}, bf16[2,32,1024]{2,1,0:T(8,128)(2,1)S(1)}, u32[]{:S(2)}, u32[]{:S(2)}) %collective-permute-start.8) | collective-permute-done | bytes 131104 | tf_op jit(solution)/shard_map/ppermute | solution.py:434
  96.6 1.2 %table.1 = f32[256,1024]{1,0:T(8,128)} custom-call(s32[1,64]{1,0:T(1,128)S(1)} %copy-done.3, s32[1,64]{1,0:T(1,128)S(1)} %collective-permute-done.refs_1_, bf16[2,32,1024]{2,1,0:T(8,128)(2,1)S(1)} %sums.5.refs_2_, bf16[2,32,1024]{2,1,0:T(8,128)(2,1)S(1)} %collective-permute-done.8.refs_3_), custom_call_target="tpu_custom_call" | custom-call | tf_op jit(solution)/shard_map/table/pallas_call | solution.py:459
  (16 shorter events, 0.2 us)
Async XLA Ops:
  5.7 7.5 %copy-start.3 = (s32[1,64]{1,0:T(1,128)S(1)}, s32[1,64]{1,0:T(1,128)}, u32[]{:S(2)}) copy-start(s32[1,64]{1,0:T(1,128)} %refs_0_.1) | copy-start | bytes 772
  5.7 30.4 %all-to-all-start = ((bf16[16,32,1024]{2,1,0:T(8,128)(2,1)}), bf16[16,32,1024]{2,1,0:T(8,128)(2,1)S(1)}, u32[]{:S(2)}, u32[]{:S(2)}) async-start(bf16[16,32,1024]{2,1,0:T(8,128)(2,1)} %bitcast.19), calls=%async_computation | async-start | bytes 2097152 | tf_op jit(solution)/shard_map/all_to_all | solution.py:397
  13.2 5.3 %copy-start.4 = (bf16[1,128,4,1024]{3,2,1,0:T(4,128)(2,1)S(1)}, bf16[1,128,4,1024]{3,2,1,0:T(4,128)(2,1)}, u32[]{:S(2)}) copy-start(bf16[1,128,4,1024]{3,2,1,0:T(4,128)(2,1)} %param.7) | copy-start | bytes 3145732
  13.2 5.7 %collective-permute-start = (s32[1,64]{1,0:T(1,128)S(1)}, s32[1,64]{1,0:T(1,128)S(1)}, u32[]{:S(2)}, u32[]{:S(2)}) collective-permute-start(s32[1,64]{1,0:T(1,128)S(1)} %copy-done.3), channel_id=1, source_target_pairs={{0,16},{16,0},{1,17},{17,1},{2,18},{18,2},{3,19},{19,3},{4,20},{20... | collective-permute-start | bytes 776 | tf_op jit(solution)/shard_map/ppermute | solution.py:350
  18.8 17.3 %copy-start.2 = (f32[8,128]{1,0:T(8,128)S(1)}, f32[8,128]{1,0:T(8,128)}, u32[]{:S(2)}) copy-start(f32[8,128]{1,0:T(8,128)} %get-tuple-element.14.refs_0_) | copy-start | bytes 12292
  40.2 31.7 %copy-start = (bf16[8,64,1024]{2,1,0:T(8,128)(2,1)S(1)}, bf16[8,64,1024]{2,1,0:T(8,128)(2,1)}, u32[]{:S(2)}) copy-start(bf16[8,64,1024]{2,1,0:T(8,128)(2,1)} %get-tuple-element.11.embedded) | copy-start | bytes 3145732
  40.2 31.7 %copy-start.1 = (bf16[8,8,64,128]{3,2,1,0:T(8,128)(2,1)S(1)}, bf16[8,8,64,128]{3,2,1,0:T(8,128)(2,1)}, u32[]{:S(2)}) copy-start(bf16[8,8,64,128]{3,2,1,0:T(8,128)(2,1)} %get-tuple-element.12.weights) | copy-start | bytes 3145732
  75.9 1.7 %collective-permute-start.1 = (bf16[32,1024]{1,0:T(8,128)(2,1)S(1)}, bf16[32,1024]{1,0:T(8,128)(2,1)S(1)}, u32[]{:S(2)}, u32[]{:S(2)}) collective-permute-start(bf16[32,1024]{1,0:T(8,128)(2,1)S(1)} %get-tuple-element.17), channel_id=1, source_target_pairs={{0,1},{1,0},{2,3},{3,2},{4,5},{5,4},{6,7},{7,6},{8,9},{9,8},{10,11... | collective-permute-start | bytes 196616 | tf_op jit(solution)/shard_map/ppermute | solution.py:434
  77.6 4.5 %collective-permute-start.2 = (bf16[32,1024]{1,0:T(8,128)(2,1)S(1)}, bf16[32,1024]{1,0:T(8,128)(2,1)S(1)}, u32[]{:S(2)}, u32[]{:S(2)}) collective-permute-start(bf16[32,1024]{1,0:T(8,128)(2,1)S(1)} %sums.3.refs_0_), channel_id=1, source_target_pairs={{0,4},{1,5},{2,6},{3,7},{4,0},{5,1},{6,2},{7,3},{8,12},{9,13},{10,... | collective-permute-start | bytes 196616 | tf_op jit(solution)/shard_map/ppermute | solution.py:434
  79.5 8.2 %collective-permute-start.3 = (bf16[32,1024]{1,0:T(8,128)(2,1)S(1)}, bf16[32,1024]{1,0:T(8,128)(2,1)S(1)}, u32[]{:S(2)}, u32[]{:S(2)}) collective-permute-start(bf16[32,1024]{1,0:T(8,128)(2,1)S(1)} %sums.3.refs_0_), channel_id=1, source_target_pairs={{0,8},{1,9},{2,10},{3,11},{4,12},{5,13},{6,14},{7,15},{8,0},{9,1},... | collective-permute-start | bytes 196616 | tf_op jit(solution)/shard_map/ppermute | solution.py:434
  80.4 7.3 %collective-permute-start.4 = (bf16[32,1024]{1,0:T(8,128)(2,1)S(1)}, bf16[32,1024]{1,0:T(8,128)(2,1)S(1)}, u32[]{:S(2)}, u32[]{:S(2)}) collective-permute-start(bf16[32,1024]{1,0:T(8,128)(2,1)S(1)} %sums.3.refs_0_), channel_id=1, source_target_pairs={{0,12},{1,13},{2,14},{3,15},{4,8},{5,9},{6,10},{7,11},{8,4},{9,5},... | collective-permute-start | bytes 196616 | tf_op jit(solution)/shard_map/ppermute | solution.py:434
  87.8 4.6 %collective-permute-start.5 = (bf16[32,1024]{1,0:T(8,128)(2,1)S(1)}, bf16[32,1024]{1,0:T(8,128)(2,1)S(1)}, u32[]{:S(2)}, u32[]{:S(2)}) collective-permute-start(bf16[32,1024]{1,0:T(8,128)(2,1)S(1)} %sums.4.refs_0_), channel_id=1, source_target_pairs={{0,2},{1,3},{2,0},{3,1},{4,6},{5,7},{6,4},{7,5},{8,10},{9,11},{10,... | collective-permute-start | bytes 196616 | tf_op jit(solution)/shard_map/ppermute | solution.py:434
  88.5 4.9 %collective-permute-start.6 = (bf16[32,1024]{1,0:T(8,128)(2,1)S(1)}, bf16[32,1024]{1,0:T(8,128)(2,1)S(1)}, u32[]{:S(2)}, u32[]{:S(2)}) collective-permute-start(bf16[32,1024]{1,0:T(8,128)(2,1)S(1)} %sums.4.refs_0_), channel_id=1, source_target_pairs={{0,16},{1,17},{2,18},{3,19},{4,20},{5,21},{6,22},{7,23},{8,24},{9,... | collective-permute-start | bytes 196616 | tf_op jit(solution)/shard_map/ppermute | solution.py:434
  90.0 5.2 %collective-permute-start.7 = (bf16[32,1024]{1,0:T(8,128)(2,1)S(1)}, bf16[32,1024]{1,0:T(8,128)(2,1)S(1)}, u32[]{:S(2)}, u32[]{:S(2)}) collective-permute-start(bf16[32,1024]{1,0:T(8,128)(2,1)S(1)} %sums.4.refs_0_), channel_id=1, source_target_pairs={{0,18},{1,19},{2,16},{3,17},{4,22},{5,23},{6,20},{7,21},{8,26},{9,... | collective-permute-start | bytes 196616 | tf_op jit(solution)/shard_map/ppermute | solution.py:434
  95.2 1.4 %collective-permute-start.8 = (bf16[2,32,1024]{2,1,0:T(8,128)(2,1)S(1)}, bf16[2,32,1024]{2,1,0:T(8,128)(2,1)S(1)}, u32[]{:S(2)}, u32[]{:S(2)}) collective-permute-start(bf16[2,32,1024]{2,1,0:T(8,128)(2,1)S(1)} %sums.5.refs_2_), channel_id=1, source_target_pairs={{0,1},{1,0},{2,3},{3,2},{4,5},{5,4},{6,7},{7,6},{8,9},{9,8},{10,11... | collective-permute-start | bytes 393224 | tf_op jit(solution)/shard_map/ppermute | solution.py:434
where the time goes:
time: 98.1 us; the launch traced here: 97.9 us
  blocking collectives  31.6 us (32%)
  waiting for transfers between devices  29 us (30%)
  Pallas kernels  18.2 us (19%)
  starting transfers between devices  17.9 us (18%)
    all_to_all x1, blocking collectives, body(): lax.all_to_all(mixed_grad, 'shard', split_axis=0, concat_axis=0, tiled=True)  31.6 us
    all_to_all x1, waiting for transfers between devices, body(): lax.all_to_all(mixed, 'shard', split_axis=0, concat_axis=0, tiled=True)  17.3 us
    ppermute x8, waiting for transfers between devices, to_partner(): return lax.ppermute(array, ('group', 'shard'), pairs_of_devices)  11.7 us
    ppermute x8, starting transfers between devices, to_partner(): return lax.ppermute(array, ('group', 'shard'), pairs_of_devices)  8.85 us
    all_to_all x1, starting transfers between devices, body(): lax.all_to_all(mixed, 'shard', split_axis=0, concat_axis=0, tiled=True)  7.49 us
    pallas_call x1, Pallas kernels, body(): pl.pallas_call(functools.partial(spatial_kernel, width), grid=(steps,), o...  5.05 us
    pallas_call x1, Pallas kernels, body(): pl.pallas_call(functools.partial(temporal_kernel, width, parts), grid=(st...  4.09 us
    pallas_call x1, Pallas kernels, body(): pl.pallas_call(functools.partial(spatial_back_kernel, width), grid=(steps...  3.98 us
  transfers between devices with their start and end apart: 10, of which 8 were waited for; matrix products, arithmetic and copies ran while one was open for 0% of the time, Pallas kernels for 4%

commit v1 on v0

--- a/solution.py
+++ b/solution.py
@@ -14,7 +14,7 @@
 MASKED = -1e30
 SUBLANES = 8
 STEP = 512
-PIECES = 4
+PIECES = 8
 PLANE = 4
 SPATIAL_GROUP = 32
 TEMPORAL_GROUP = 8
@@ -163,8 +163,12 @@
     @pl.when(pl.program_id(0) == 0)
     def _():
         bias[...] = pair_bias(counts, offsets, slots)
-        chosen = lax.broadcasted_iota(jnp.int32, (templates, slots), 0) == layout[...]
-        spread[...] = jnp.transpose(chosen.astype(jnp.float32)).astype(jnp.bfloat16)
+        wanted = jnp.broadcast_to(layout[...].astype(jnp.float32), (LANES, slots))
+        wanted = jnp.transpose(wanted).astype(jnp.int32)
+        template = lax.broadcasted_iota(jnp.int32, (slots, LANES), 1)
+        for first in range(0, templates, LANES):
+            chosen = wanted == template + first
+            spread[:, pl.ds(first, LANES)] = chosen.astype(jnp.float32).astype(jnp.bfloat16)
 
     chosen_rows = dot(spread[...], embedding[...], (1, 0))
     rows[...] = chosen_rows.astype(jnp.bfloat16)
@@ -448,7 +452,7 @@
     total = summed(
         far_sum_kernel,
         (half, model),
-        [to_partner(halved, 0, far * PLANE) for far in range(far_count)],
+        [to_partner(halved, 0, far * PLANE) for far in reversed(range(far_count))][::-1],
         [pltpu.VMEM((far_count, half, model), jnp.float32)],
     )
     crossed = [

time: 98.1 us -> 98.1 us (level)
  no operation moved by 1% of the time
where the time goes in v1:
time: 98.1 us; the launch traced here: 97.8 us
  blocking collectives  31.6 us (32%)
  waiting for transfers between devices  29 us (30%)
  Pallas kernels  18.2 us (19%)
  starting transfers between devices  17.9 us (18%)
    all_to_all x1, blocking collectives, body(): lax.all_to_all(mixed_grad, 'shard', split_axis=0, concat_axis=0, tiled=True)  31.6 us
    all_to_all x1, waiting for transfers between devices, body(): lax.all_to_all(mixed, 'shard', split_axis=0, concat_axis=0, tiled=True)  17.3 us
    ppermute x8, waiting for transfers between devices, to_partner(): return lax.ppermute(array, ('group', 'shard'), pairs_of_devices)  11.7 us
    ppermute x8, starting transfers between devices, to_partner(): return lax.ppermute(array, ('group', 'shard'), pairs_of_devices)  8.85 us
    all_to_all x1, starting transfers between devices, body(): lax.all_to_all(mixed, 'shard', split_axis=0, concat_axis=0, tiled=True)  7.49 us
    pallas_call x1, Pallas kernels, body(): pl.pallas_call(functools.partial(spatial_kernel, width), grid=(steps,), o...  5.04 us
    pallas_call x1, Pallas kernels, body(): pl.pallas_call(functools.partial(temporal_kernel, width, parts), grid=(st...  4.1 us
    pallas_call x1, Pallas kernels, body(): pl.pallas_call(functools.partial(spatial_back_kernel, width), grid=(steps...  3.98 us
  transfers between devices with their start and end apart: 10, of which 8 were waited for; matrix products, arithmetic and copies ran while one was open for 0% of the time, Pallas kernels for 4%

profile of v1, /device:TPU:0, one launch (start us, length us, event | category | flops | bytes accessed | tf_op | source)
XLA Modules:
  0.0 97.8 jit_solution(14728227711293515498)
XLA Ops:
  0.6 5.0 %spatial.1 = (bf16[64,1024]{1,0:T(8,128)(2,1)}, bf16[512,1024]{1,0:T(8,128)(2,1)}) custom-call(s32[1,2]{1,0:T(1,128)} %counts.3, s32[1,2]{1,0:T(1,128)} %offsets.3, s32[1,64]{1,0:T(1,128)} %refs_0_.1, bf16[512,1024]{1,0:T(8,128)(2,1)} %embedding.1, bf16[8,64,1024]{2,1,0:T(8,128)(2,1)} %bitcast.16), custom_call_target="tpu_custom_call" | custom-call | tf_op jit(solution)/shard_map/spatial/pallas_call | solution.py:369
  5.7 7.5 %all-to-all-start = ((bf16[16,32,1024]{2,1,0:T(8,128)(2,1)}), bf16[16,32,1024]{2,1,0:T(8,128)(2,1)S(1)}, u32[]{:S(2)}, u32[]{:S(2)}) async-start(bf16[16,32,1024]{2,1,0:T(8,128)(2,1)} %bitcast.19), calls=%async_computation | async-start | bytes 2097152 | tf_op jit(solution)/shard_map/all_to_all | solution.py:401
  13.2 1.6 %collective-permute-start = (s32[1,64]{1,0:T(1,128)S(1)}, s32[1,64]{1,0:T(1,128)S(1)}, u32[]{:S(2)}, u32[]{:S(2)}) collective-permute-start(s32[1,64]{1,0:T(1,128)S(1)} %copy-done.3), channel_id=1, source_target_pairs={{0,16},{16,0},{1,17},{17,1},{2,18},{18,2},{3,19},{19,3},{4,20},{20... | collective-permute-start | bytes 776 | tf_op jit(solution)/shard_map/ppermute | solution.py:354
  14.8 3.7 %weights.1 = (bf16[8,64,1024]{2,1,0:T(8,128)(2,1)}, bf16[8,8,64,128]{3,2,1,0:T(8,128)(2,1)}, f32[8,128]{1,0:T(8,128)}) custom-call(s32[1,2]{1,0:T(1,128)} %counts.3, s32[1,2]{1,0:T(1,128)} %offsets.3, bf16[64,1024]{1,0:T(8,128)(2,1)} %get-tuple-element.10.rows, bf16[8,64,1024]{2,1,0:T(8,128)(2,1)} %bitcast.17), custom_call_target="tpu_custom_call" | custom-call | flops 134217728 | bytes 3145728 | tf_op jit(solution)/shard_map/weights/pallas_call | solution.py:383
  18.5 0.3 copy.10
  18.9 17.3 %all-to-all-done = bf16[16,32,1024]{2,1,0:T(8,128)(2,1)S(1)} async-done(((bf16[16,32,1024]{2,1,0:T(8,128)(2,1)}), bf16[16,32,1024]{2,1,0:T(8,128)(2,1)S(1)}, u32[]{:S(2)}, u32[]{:S(2)}) %all-to-all-start) | async-done | bytes 1048608 | tf_op jit(solution)/shard_map/all_to_all | solution.py:401
  36.1 4.1 %temporal.1 = bf16[512,1024]{1,0:T(8,128)(2,1)S(1)} custom-call(bf16[512,1024]{1,0:T(8,128)(2,1)S(1)} %bitcast.13, bf16[4,128,1024]{2,1,0:T(8,128)(2,1)S(1)} %bitcast.14, f32[8,128]{1,0:T(8,128)S(1)} %copy-done.2, s32[1,64]{1,0:T(1,128)S(1)} %collective-permute-done.refs_1_), custom_call_target="tpu_custom_call" | custom-call | tf_op jit(solution)/shard_map/temporal/pallas_call | solution.py:402
  40.2 31.6 %all_to_all.22 = bf16[16,32,1024]{2,1,0:T(8,128)(2,1)S(1)} all-to-all(bf16[16,32,1024]{2,1,0:T(8,128)(2,1)S(1)} %bitcast.15), channel_id=1, replica_groups=mesh['group'=2,'shard'=16] {'shard'}, dimensions={0} | all-to-all | bytes 2097152 | tf_op jit(solution)/shard_map/all_to_all | solution.py:414
  71.9 4.0 %spatial_back.1 = (bf16[8,64,1024]{2,1,0:T(8,128)(2,1)}, bf16[32,1024]{1,0:T(8,128)(2,1)S(1)}, bf16[32,1024]{1,0:T(8,128)(2,1)S(1)}) custom-call(bf16[8,64,1024]{2,1,0:T(8,128)(2,1)S(1)} %copy-done, bf16[8,8,64,128]{3,2,1,0:T(8,128)(2,1)S(1)} %copy-done.1, bf16[512,1024]{1,0:T(8,128)(2,1)S(1)} %bitcast.12), custom_call_target="tpu_custom_call" | custom-call | tf_op jit(solution)/shard_map/spatial_back/pallas_call | solution.py:416
  75.9 0.8 collective-permute-start.1
  76.6 0.9 collective-permute-done.1.arrived
  77.6 1.9 %collective-permute-start.2 = (bf16[32,1024]{1,0:T(8,128)(2,1)S(1)}, bf16[32,1024]{1,0:T(8,128)(2,1)S(1)}, u32[]{:S(2)}, u32[]{:S(2)}) collective-permute-start(bf16[32,1024]{1,0:T(8,128)(2,1)S(1)} %sums.3.refs_0_), channel_id=1, source_target_pairs={{0,4},{1,5},{2,6},{3,7},{4,0},{5,1},{6,2},{7,3},{8,12},{9,13},{10,... | collective-permute-start | bytes 196616 | tf_op jit(solution)/shard_map/ppermute | solution.py:438
  79.5 0.9 collective-permute-start.3
  80.4 1.6 %collective-permute-start.4 = (bf16[32,1024]{1,0:T(8,128)(2,1)S(1)}, bf16[32,1024]{1,0:T(8,128)(2,1)S(1)}, u32[]{:S(2)}, u32[]{:S(2)}) collective-permute-start(bf16[32,1024]{1,0:T(8,128)(2,1)S(1)} %sums.3.refs_0_), channel_id=1, source_target_pairs={{0,12},{1,13},{2,14},{3,15},{4,8},{5,9},{6,10},{7,11},{8,4},{9,5},... | collective-permute-start | bytes 196616 | tf_op jit(solution)/shard_map/ppermute | solution.py:438
  82.1 5.6 %collective-permute-done.3.refs_2_ = bf16[32,1024]{1,0:T(8,128)(2,1)S(1)} collective-permute-done((bf16[32,1024]{1,0:T(8,128)(2,1)S(1)}, bf16[32,1024]{1,0:T(8,128)(2,1)S(1)}, u32[]{:S(2)}, u32[]{:S(2)}) %collective-permute-start.3) | collective-permute-done | bytes 65568 | tf_op jit(solution)/shard_map/ppermute | solution.py:438
  87.8 0.7 collective-permute-start.5
  88.5 1.5 %collective-permute-start.6 = (bf16[32,1024]{1,0:T(8,128)(2,1)S(1)}, bf16[32,1024]{1,0:T(8,128)(2,1)S(1)}, u32[]{:S(2)}, u32[]{:S(2)}) collective-permute-start(bf16[32,1024]{1,0:T(8,128)(2,1)S(1)} %sums.4.refs_0_), channel_id=1, source_target_pairs={{0,16},{1,17},{2,18},{3,19},{4,20},{5,21},{6,22},{7,23},{8,24},{9,... | collective-permute-start | bytes 196616 | tf_op jit(solution)/shard_map/ppermute | solution.py:438
  90.0 1.4 %collective-permute-start.7 = (bf16[32,1024]{1,0:T(8,128)(2,1)S(1)}, bf16[32,1024]{1,0:T(8,128)(2,1)S(1)}, u32[]{:S(2)}, u32[]{:S(2)}) collective-permute-start(bf16[32,1024]{1,0:T(8,128)(2,1)S(1)} %sums.4.refs_0_), channel_id=1, source_target_pairs={{0,18},{1,19},{2,16},{3,17},{4,22},{5,23},{6,20},{7,21},{8,26},{9,... | collective-permute-start | bytes 196616 | tf_op jit(solution)/shard_map/ppermute | solution.py:438
  91.4 1.1 %collective-permute-done.5.refs_1_ = bf16[32,1024]{1,0:T(8,128)(2,1)S(1)} collective-permute-done((bf16[32,1024]{1,0:T(8,128)(2,1)S(1)}, bf16[32,1024]{1,0:T(8,128)(2,1)S(1)}, u32[]{:S(2)}, u32[]{:S(2)}) %collective-permute-start.5) | collective-permute-done | bytes 65568 | tf_op jit(solution)/shard_map/ppermute | solution.py:438
  92.4 1.0 collective-permute-done.6.refs_2_
  93.4 1.8 %collective-permute-done.7.refs_3_ = bf16[32,1024]{1,0:T(8,128)(2,1)S(1)} collective-permute-done((bf16[32,1024]{1,0:T(8,128)(2,1)S(1)}, bf16[32,1024]{1,0:T(8,128)(2,1)S(1)}, u32[]{:S(2)}, u32[]{:S(2)}) %collective-permute-start.7) | collective-permute-done | bytes 65568 | tf_op jit(solution)/shard_map/ppermute | solution.py:438
  95.2 0.1 collective-permute-start.8
  95.3 1.3 %collective-permute-done.8.refs_3_ = bf16[2,32,1024]{2,1,0:T(8,128)(2,1)S(1)} collective-permute-done((bf16[2,32,1024]{2,1,0:T(8,128)(2,1)S(1)}, bf16[2,32,1024]{2,1,0:T(8,128)(2,1)S(1)}, u32[]{:S(2)}, u32[]{:S(2)}) %collective-permute-start.8) | collective-permute-done | bytes 131104 | tf_op jit(solution)/shard_map/ppermute | solution.py:438
  96.6 1.2 %table.1 = f32[256,1024]{1,0:T(8,128)} custom-call(s32[1,64]{1,0:T(1,128)S(1)} %copy-done.3, s32[1,64]{1,0:T(1,128)S(1)} %collective-permute-done.refs_1_, bf16[2,32,1024]{2,1,0:T(8,128)(2,1)S(1)} %sums.5.refs_2_, bf16[2,32,1024]{2,1,0:T(8,128)(2,1)S(1)} %collective-permute-done.8.refs_3_), custom_call_target="tpu_custom_call" | custom-call | tf_op jit(solution)/shard_map/table/pallas_call | solution.py:463
  (16 shorter events, 0.2 us)
Async XLA Ops:
  5.7 7.5 %copy-start.3 = (s32[1,64]{1,0:T(1,128)S(1)}, s32[1,64]{1,0:T(1,128)}, u32[]{:S(2)}) copy-start(s32[1,64]{1,0:T(1,128)} %refs_0_.1) | copy-start | bytes 772
  5.7 30.4 %all-to-all-start = ((bf16[16,32,1024]{2,1,0:T(8,128)(2,1)}), bf16[16,32,1024]{2,1,0:T(8,128)(2,1)S(1)}, u32[]{:S(2)}, u32[]{:S(2)}) async-start(bf16[16,32,1024]{2,1,0:T(8,128)(2,1)} %bitcast.19), calls=%async_computation | async-start | bytes 2097152 | tf_op jit(solution)/shard_map/all_to_all | solution.py:401
  13.2 5.3 %copy-start.4 = (bf16[1,128,4,1024]{3,2,1,0:T(4,128)(2,1)S(1)}, bf16[1,128,4,1024]{3,2,1,0:T(4,128)(2,1)}, u32[]{:S(2)}) copy-start(bf16[1,128,4,1024]{3,2,1,0:T(4,128)(2,1)} %param.7) | copy-start | bytes 3145732
  13.2 5.7 %collective-permute-start = (s32[1,64]{1,0:T(1,128)S(1)}, s32[1,64]{1,0:T(1,128)S(1)}, u32[]{:S(2)}, u32[]{:S(2)}) collective-permute-start(s32[1,64]{1,0:T(1,128)S(1)} %copy-done.3), channel_id=1, source_target_pairs={{0,16},{16,0},{1,17},{17,1},{2,18},{18,2},{3,19},{19,3},{4,20},{20... | collective-permute-start | bytes 776 | tf_op jit(solution)/shard_map/ppermute | solution.py:354
  18.8 17.3 %copy-start.2 = (f32[8,128]{1,0:T(8,128)S(1)}, f32[8,128]{1,0:T(8,128)}, u32[]{:S(2)}) copy-start(f32[8,128]{1,0:T(8,128)} %get-tuple-element.14.refs_0_) | copy-start | bytes 12292
  40.2 31.7 %copy-start = (bf16[8,64,1024]{2,1,0:T(8,128)(2,1)S(1)}, bf16[8,64,1024]{2,1,0:T(8,128)(2,1)}, u32[]{:S(2)}) copy-start(bf16[8,64,1024]{2,1,0:T(8,128)(2,1)} %get-tuple-element.11.embedded) | copy-start | bytes 3145732
  40.2 31.7 %copy-start.1 = (bf16[8,8,64,128]{3,2,1,0:T(8,128)(2,1)S(1)}, bf16[8,8,64,128]{3,2,1,0:T(8,128)(2,1)}, u32[]{:S(2)}) copy-start(bf16[8,8,64,128]{3,2,1,0:T(8,128)(2,1)} %get-tuple-element.12.weights) | copy-start | bytes 3145732
  75.9 1.7 %collective-permute-start.1 = (bf16[32,1024]{1,0:T(8,128)(2,1)S(1)}, bf16[32,1024]{1,0:T(8,128)(2,1)S(1)}, u32[]{:S(2)}, u32[]{:S(2)}) collective-permute-start(bf16[32,1024]{1,0:T(8,128)(2,1)S(1)} %get-tuple-element.17), channel_id=1, source_target_pairs={{0,1},{1,0},{2,3},{3,2},{4,5},{5,4},{6,7},{7,6},{8,9},{9,8},{10,11... | collective-permute-start | bytes 196616 | tf_op jit(solution)/shard_map/ppermute | solution.py:438
  77.6 4.5 %collective-permute-start.2 = (bf16[32,1024]{1,0:T(8,128)(2,1)S(1)}, bf16[32,1024]{1,0:T(8,128)(2,1)S(1)}, u32[]{:S(2)}, u32[]{:S(2)}) collective-permute-start(bf16[32,1024]{1,0:T(8,128)(2,1)S(1)} %sums.3.refs_0_), channel_id=1, source_target_pairs={{0,4},{1,5},{2,6},{3,7},{4,0},{5,1},{6,2},{7,3},{8,12},{9,13},{10,... | collective-permute-start | bytes 196616 | tf_op jit(solution)/shard_map/ppermute | solution.py:438
  79.5 8.2 %collective-permute-start.3 = (bf16[32,1024]{1,0:T(8,128)(2,1)S(1)}, bf16[32,1024]{1,0:T(8,128)(2,1)S(1)}, u32[]{:S(2)}, u32[]{:S(2)}) collective-permute-start(bf16[32,1024]{1,0:T(8,128)(2,1)S(1)} %sums.3.refs_0_), channel_id=1, source_target_pairs={{0,8},{1,9},{2,10},{3,11},{4,12},{5,13},{6,14},{7,15},{8,0},{9,1},... | collective-permute-start | bytes 196616 | tf_op jit(solution)/shard_map/ppermute | solution.py:438
  80.4 7.3 %collective-permute-start.4 = (bf16[32,1024]{1,0:T(8,128)(2,1)S(1)}, bf16[32,1024]{1,0:T(8,128)(2,1)S(1)}, u32[]{:S(2)}, u32[]{:S(2)}) collective-permute-start(bf16[32,1024]{1,0:T(8,128)(2,1)S(1)} %sums.3.refs_0_), channel_id=1, source_target_pairs={{0,12},{1,13},{2,14},{3,15},{4,8},{5,9},{6,10},{7,11},{8,4},{9,5},... | collective-permute-start | bytes 196616 | tf_op jit(solution)/shard_map/ppermute | solution.py:438
  87.8 4.6 %collective-permute-start.5 = (bf16[32,1024]{1,0:T(8,128)(2,1)S(1)}, bf16[32,1024]{1,0:T(8,128)(2,1)S(1)}, u32[]{:S(2)}, u32[]{:S(2)}) collective-permute-start(bf16[32,1024]{1,0:T(8,128)(2,1)S(1)} %sums.4.refs_0_), channel_id=1, source_target_pairs={{0,2},{1,3},{2,0},{3,1},{4,6},{5,7},{6,4},{7,5},{8,10},{9,11},{10,... | collective-permute-start | bytes 196616 | tf_op jit(solution)/shard_map/ppermute | solution.py:438
  88.5 4.9 %collective-permute-start.6 = (bf16[32,1024]{1,0:T(8,128)(2,1)S(1)}, bf16[32,1024]{1,0:T(8,128)(2,1)S(1)}, u32[]{:S(2)}, u32[]{:S(2)}) collective-permute-start(bf16[32,1024]{1,0:T(8,128)(2,1)S(1)} %sums.4.refs_0_), channel_id=1, source_target_pairs={{0,16},{1,17},{2,18},{3,19},{4,20},{5,21},{6,22},{7,23},{8,24},{9,... | collective-permute-start | bytes 196616 | tf_op jit(solution)/shard_map/ppermute | solution.py:438
  90.0 5.2 %collective-permute-start.7 = (bf16[32,1024]{1,0:T(8,128)(2,1)S(1)}, bf16[32,1024]{1,0:T(8,128)(2,1)S(1)}, u32[]{:S(2)}, u32[]{:S(2)}) collective-permute-start(bf16[32,1024]{1,0:T(8,128)(2,1)S(1)} %sums.4.refs_0_), channel_id=1, source_target_pairs={{0,18},{1,19},{2,16},{3,17},{4,22},{5,23},{6,20},{7,21},{8,26},{9,... | collective-permute-start | bytes 196616 | tf_op jit(solution)/shard_map/ppermute | solution.py:438
  95.2 1.4 %collective-permute-start.8 = (bf16[2,32,1024]{2,1,0:T(8,128)(2,1)S(1)}, bf16[2,32,1024]{2,1,0:T(8,128)(2,1)S(1)}, u32[]{:S(2)}, u32[]{:S(2)}) collective-permute-start(bf16[2,32,1024]{2,1,0:T(8,128)(2,1)S(1)} %sums.5.refs_2_), channel_id=1, source_target_pairs={{0,1},{1,0},{2,3},{3,2},{4,5},{5,4},{6,7},{7,6},{8,9},{9,8},{10,11... | collective-permute-start | bytes 393224 | tf_op jit(solution)/shard_map/ppermute | solution.py:438

commit v2 on v1

--- a/solution.py
+++ b/solution.py
@@ -131,6 +131,11 @@
     return pl.ds(pair * LANES, LANES)
 
 
+def step_columns(pair, width):
+    start = pl.program_id(0) * width + pair * LANES
+    return pl.ds(pl.multiple_of(start, LANES), LANES)
+
+
 def in_groups(pairs, rows, size):
     items = [(pair, row) for pair in range(pairs) for row in range(rows)]
     return [items[start : start + size] for start in range(0, len(items), size)]
@@ -210,13 +215,14 @@
 
 def temporal_kernel(width, parts, mixed, out_grad, *refs):
     mixed_grad, received, returned = refs[-3:]
-    electrodes, patches, model = out_grad.shape
+    electrodes, patches, _ = out_grad.shape
+    model = mixed_grad.shape[1]
     local = patches // parts
     pairs = model // LANES
     score_masks = head_masks(width, 0.5 / math.sqrt(width))
     ones = head_masks(width, 1.0)
     for pair in range(pairs):
-        received[pair] = mixed[:, pair_columns(pair)].astype(jnp.float32)
+        received[pair] = mixed[:, step_columns(pair, model)].astype(jnp.float32)
     for group in in_groups(pairs, electrodes, TEMPORAL_GROUP):
         places = [electrode_rows(e, electrodes, parts, local) for _, e in group]
         values = each(
@@ -226,7 +232,7 @@
             group,
             places,
         )
-        cotangents = [out_grad[e, :, pair_columns(pair)] for pair, e in group]
+        cotangents = [out_grad[e, :, step_columns(pair, model)] for pair, e in group]
         scaled = each(lambda v: head_rows(v, score_masks), values)
         scores = each(lambda v, s: dot(v, s, (1, 1)), values, scaled)
         heads_grads = each(lambda g: head_rows(g, ones), cotangents)
@@ -255,7 +261,7 @@
     ones = head_masks(width, 1.0)
     totals = [jnp.zeros((slots, LANES), jnp.float32) for _ in range(pairs)]
     for pair in range(pairs):
-        received[pair] = mixed_grad[:, pair_columns(pair)].astype(jnp.float32)
+        received[pair] = mixed_grad[:, step_columns(pair, model)].astype(jnp.float32)
     for group in in_groups(pairs, patches, SPATIAL_GROUP):
         cotangents = [
             received[pair, of_patch(p, slots, patches), :].astype(jnp.bfloat16)
@@ -403,7 +409,7 @@
         functools.partial(temporal_kernel, width, parts),
         grid=(steps,),
         out_shape=flat_shape,
-        in_specs=[flat, pl.BlockSpec((own, patches, STEP), lambda step: (0, 0, step))]
+        in_specs=[VMEM, VMEM]
         + [pl.BlockSpec(memory_space=pl.ANY)] * groups,
         out_specs=flat,
         scratch_shapes=[flat_scratch, flat_scratch],
@@ -417,7 +423,7 @@
         functools.partial(spatial_back_kernel, width),
         grid=(steps,),
         out_shape=(plane_shape,) + (jax.ShapeDtypeStruct((half, model), jnp.bfloat16),) * 2,
-        in_specs=[planes, squares, flat],
+        in_specs=[planes, squares, VMEM],
         out_specs=(planes,) + (pl.BlockSpec((half, STEP), lambda step: (0, step)),) * 2,
         scratch_shapes=[pltpu.VMEM((pairs, slots, LANES), jnp.float32), flat_scratch],
         compiler_params=PARAMS,

time: 98.1 us -> 98 us (level)
  no operation moved by 1% of the time
where the time goes in v2:
time: 98 us; the launch traced here: 97.7 us
  blocking collectives  31.6 us (32%)
  waiting for transfers between devices  29 us (30%)
  Pallas kernels  18.1 us (18%)
  starting transfers between devices  17.9 us (18%)
    all_to_all x1, blocking collectives, body(): lax.all_to_all(mixed_grad, 'shard', split_axis=0, concat_axis=0, tiled=True)  31.6 us
    all_to_all x1, waiting for transfers between devices, body(): lax.all_to_all(mixed, 'shard', split_axis=0, concat_axis=0, tiled=True)  17.3 us
    ppermute x8, waiting for transfers between devices, to_partner(): return lax.ppermute(array, ('group', 'shard'), pairs_of_devices)  11.8 us
    ppermute x8, starting transfers between devices, to_partner(): return lax.ppermute(array, ('group', 'shard'), pairs_of_devices)  8.85 us
    all_to_all x1, starting transfers between devices, body(): lax.all_to_all(mixed, 'shard', split_axis=0, concat_axis=0, tiled=True)  7.49 us
    pallas_call x1, Pallas kernels, body(): pl.pallas_call(functools.partial(spatial_kernel, width), grid=(steps,), o...  5.04 us
    pallas_call x1, Pallas kernels, body(): pl.pallas_call(functools.partial(temporal_kernel, width, parts), grid=(st...  3.99 us
    pallas_call x1, Pallas kernels, body(): pl.pallas_call(functools.partial(spatial_back_kernel, width), grid=(steps...  3.97 us
  transfers between devices with their start and end apart: 10, of which 8 were waited for; matrix products, arithmetic and copies ran while one was open for 0% of the time, Pallas kernels for 4%

profile of v2, /device:TPU:0, one launch (start us, length us, event | category | flops | bytes accessed | tf_op | source)
XLA Modules:
  0.0 97.7 jit_solution(17475980204949669560)
XLA Ops:
  0.6 5.0 %spatial.1 = (bf16[64,1024]{1,0:T(8,128)(2,1)}, bf16[512,1024]{1,0:T(8,128)(2,1)}) custom-call(s32[1,2]{1,0:T(1,128)} %counts.3, s32[1,2]{1,0:T(1,128)} %offsets.3, s32[1,64]{1,0:T(1,128)} %refs_0_.1, bf16[512,1024]{1,0:T(8,128)(2,1)} %embedding.1, bf16[8,64,1024]{2,1,0:T(8,128)(2,1)} %bitcast.16), custom_call_target="tpu_custom_call" | custom-call | tf_op jit(solution)/shard_map/spatial/pallas_call | solution.py:375
  5.7 7.5 %all-to-all-start = ((bf16[16,32,1024]{2,1,0:T(8,128)(2,1)}), bf16[16,32,1024]{2,1,0:T(8,128)(2,1)S(1)}, u32[]{:S(2)}, u32[]{:S(2)}) async-start(bf16[16,32,1024]{2,1,0:T(8,128)(2,1)} %bitcast.19), calls=%async_computation | async-start | bytes 2097152 | tf_op jit(solution)/shard_map/all_to_all | solution.py:407
  13.2 1.6 %collective-permute-start = (s32[1,64]{1,0:T(1,128)S(1)}, s32[1,64]{1,0:T(1,128)S(1)}, u32[]{:S(2)}, u32[]{:S(2)}) collective-permute-start(s32[1,64]{1,0:T(1,128)S(1)} %copy-done.3), channel_id=1, source_target_pairs={{0,16},{16,0},{1,17},{17,1},{2,18},{18,2},{3,19},{19,3},{4,20},{20... | collective-permute-start | bytes 776 | tf_op jit(solution)/shard_map/ppermute | solution.py:360
  14.8 3.7 %weights.1 = (bf16[8,64,1024]{2,1,0:T(8,128)(2,1)}, bf16[8,8,64,128]{3,2,1,0:T(8,128)(2,1)}, f32[8,128]{1,0:T(8,128)}) custom-call(s32[1,2]{1,0:T(1,128)} %counts.3, s32[1,2]{1,0:T(1,128)} %offsets.3, bf16[64,1024]{1,0:T(8,128)(2,1)} %get-tuple-element.10.rows, bf16[8,64,1024]{2,1,0:T(8,128)(2,1)} %bitcast.17), custom_call_target="tpu_custom_call" | custom-call | flops 134217728 | bytes 3145728 | tf_op jit(solution)/shard_map/weights/pallas_call | solution.py:389
  18.5 0.3 copy.10
  18.9 17.3 %all-to-all-done = bf16[16,32,1024]{2,1,0:T(8,128)(2,1)S(1)} async-done(((bf16[16,32,1024]{2,1,0:T(8,128)(2,1)}), bf16[16,32,1024]{2,1,0:T(8,128)(2,1)S(1)}, u32[]{:S(2)}, u32[]{:S(2)}) %all-to-all-start) | async-done | bytes 1048608 | tf_op jit(solution)/shard_map/all_to_all | solution.py:407
  36.1 4.0 %temporal.1 = bf16[512,1024]{1,0:T(8,128)(2,1)S(1)} custom-call(bf16[512,1024]{1,0:T(8,128)(2,1)S(1)} %bitcast.13, bf16[4,128,1024]{2,1,0:T(8,128)(2,1)S(1)} %bitcast.14, f32[8,128]{1,0:T(8,128)S(1)} %copy-done.2, s32[1,64]{1,0:T(1,128)S(1)} %collective-permute-done.refs_1_), custom_call_target="tpu_custom_call" | custom-call | tf_op jit(solution)/shard_map/temporal/pallas_call | solution.py:408
  40.1 31.6 %all_to_all.22 = bf16[16,32,1024]{2,1,0:T(8,128)(2,1)S(1)} all-to-all(bf16[16,32,1024]{2,1,0:T(8,128)(2,1)S(1)} %bitcast.15), channel_id=1, replica_groups=mesh['group'=2,'shard'=16] {'shard'}, dimensions={0} | all-to-all | bytes 2097152 | tf_op jit(solution)/shard_map/all_to_all | solution.py:420
  71.8 4.0 %spatial_back.1 = (bf16[8,64,1024]{2,1,0:T(8,128)(2,1)}, bf16[32,1024]{1,0:T(8,128)(2,1)S(1)}, bf16[32,1024]{1,0:T(8,128)(2,1)S(1)}) custom-call(bf16[8,64,1024]{2,1,0:T(8,128)(2,1)S(1)} %copy-done, bf16[8,8,64,128]{3,2,1,0:T(8,128)(2,1)S(1)} %copy-done.1, bf16[512,1024]{1,0:T(8,128)(2,1)S(1)} %bitcast.12), custom_call_target="tpu_custom_call" | custom-call | tf_op jit(solution)/shard_map/spatial_back/pallas_call | solution.py:422
  75.7 0.8 collective-permute-start.1
  76.5 0.9 collective-permute-done.1.arrived
  77.4 1.9 %collective-permute-start.2 = (bf16[32,1024]{1,0:T(8,128)(2,1)S(1)}, bf16[32,1024]{1,0:T(8,128)(2,1)S(1)}, u32[]{:S(2)}, u32[]{:S(2)}) collective-permute-start(bf16[32,1024]{1,0:T(8,128)(2,1)S(1)} %sums.3.refs_0_), channel_id=1, source_target_pairs={{0,4},{1,5},{2,6},{3,7},{4,0},{5,1},{6,2},{7,3},{8,12},{9,13},{10,... | collective-permute-start | bytes 196616 | tf_op jit(solution)/shard_map/ppermute | solution.py:444
  79.4 0.9 collective-permute-start.3
  80.3 1.6 %collective-permute-start.4 = (bf16[32,1024]{1,0:T(8,128)(2,1)S(1)}, bf16[32,1024]{1,0:T(8,128)(2,1)S(1)}, u32[]{:S(2)}, u32[]{:S(2)}) collective-permute-start(bf16[32,1024]{1,0:T(8,128)(2,1)S(1)} %sums.3.refs_0_), channel_id=1, source_target_pairs={{0,12},{1,13},{2,14},{3,15},{4,8},{5,9},{6,10},{7,11},{8,4},{9,5},... | collective-permute-start | bytes 196616 | tf_op jit(solution)/shard_map/ppermute | solution.py:444
  82.0 5.6 %collective-permute-done.3.refs_2_ = bf16[32,1024]{1,0:T(8,128)(2,1)S(1)} collective-permute-done((bf16[32,1024]{1,0:T(8,128)(2,1)S(1)}, bf16[32,1024]{1,0:T(8,128)(2,1)S(1)}, u32[]{:S(2)}, u32[]{:S(2)}) %collective-permute-start.3) | collective-permute-done | bytes 65568 | tf_op jit(solution)/shard_map/ppermute | solution.py:444
  87.7 0.7 collective-permute-start.5
  88.4 1.5 %collective-permute-start.6 = (bf16[32,1024]{1,0:T(8,128)(2,1)S(1)}, bf16[32,1024]{1,0:T(8,128)(2,1)S(1)}, u32[]{:S(2)}, u32[]{:S(2)}) collective-permute-start(bf16[32,1024]{1,0:T(8,128)(2,1)S(1)} %sums.4.refs_0_), channel_id=1, source_target_pairs={{0,16},{1,17},{2,18},{3,19},{4,20},{5,21},{6,22},{7,23},{8,24},{9,... | collective-permute-start | bytes 196616 | tf_op jit(solution)/shard_map/ppermute | solution.py:444
  89.9 1.4 %collective-permute-start.7 = (bf16[32,1024]{1,0:T(8,128)(2,1)S(1)}, bf16[32,1024]{1,0:T(8,128)(2,1)S(1)}, u32[]{:S(2)}, u32[]{:S(2)}) collective-permute-start(bf16[32,1024]{1,0:T(8,128)(2,1)S(1)} %sums.4.refs_0_), channel_id=1, source_target_pairs={{0,18},{1,19},{2,16},{3,17},{4,22},{5,23},{6,20},{7,21},{8,26},{9,... | collective-permute-start | bytes 196616 | tf_op jit(solution)/shard_map/ppermute | solution.py:444
  91.2 1.1 %collective-permute-done.5.refs_1_ = bf16[32,1024]{1,0:T(8,128)(2,1)S(1)} collective-permute-done((bf16[32,1024]{1,0:T(8,128)(2,1)S(1)}, bf16[32,1024]{1,0:T(8,128)(2,1)S(1)}, u32[]{:S(2)}, u32[]{:S(2)}) %collective-permute-start.5) | collective-permute-done | bytes 65568 | tf_op jit(solution)/shard_map/ppermute | solution.py:444
  92.3 1.0 collective-permute-done.6.refs_2_
  93.3 1.8 %collective-permute-done.7.refs_3_ = bf16[32,1024]{1,0:T(8,128)(2,1)S(1)} collective-permute-done((bf16[32,1024]{1,0:T(8,128)(2,1)S(1)}, bf16[32,1024]{1,0:T(8,128)(2,1)S(1)}, u32[]{:S(2)}, u32[]{:S(2)}) %collective-permute-start.7) | collective-permute-done | bytes 65568 | tf_op jit(solution)/shard_map/ppermute | solution.py:444
  95.1 0.1 collective-permute-start.8
  95.2 1.3 %collective-permute-done.8.refs_3_ = bf16[2,32,1024]{2,1,0:T(8,128)(2,1)S(1)} collective-permute-done((bf16[2,32,1024]{2,1,0:T(8,128)(2,1)S(1)}, bf16[2,32,1024]{2,1,0:T(8,128)(2,1)S(1)}, u32[]{:S(2)}, u32[]{:S(2)}) %collective-permute-start.8) | collective-permute-done | bytes 131104 | tf_op jit(solution)/shard_map/ppermute | solution.py:444
  96.5 1.2 %table.1 = f32[256,1024]{1,0:T(8,128)} custom-call(s32[1,64]{1,0:T(1,128)S(1)} %copy-done.3, s32[1,64]{1,0:T(1,128)S(1)} %collective-permute-done.refs_1_, bf16[2,32,1024]{2,1,0:T(8,128)(2,1)S(1)} %sums.5.refs_2_, bf16[2,32,1024]{2,1,0:T(8,128)(2,1)S(1)} %collective-permute-done.8.refs_3_), custom_call_target="tpu_custom_call" | custom-call | tf_op jit(solution)/shard_map/table/pallas_call | solution.py:469
  (16 shorter events, 0.2 us)
Async XLA Ops:
  5.7 7.5 %copy-start.3 = (s32[1,64]{1,0:T(1,128)S(1)}, s32[1,64]{1,0:T(1,128)}, u32[]{:S(2)}) copy-start(s32[1,64]{1,0:T(1,128)} %refs_0_.1) | copy-start | bytes 772
  5.7 30.4 %all-to-all-start = ((bf16[16,32,1024]{2,1,0:T(8,128)(2,1)}), bf16[16,32,1024]{2,1,0:T(8,128)(2,1)S(1)}, u32[]{:S(2)}, u32[]{:S(2)}) async-start(bf16[16,32,1024]{2,1,0:T(8,128)(2,1)} %bitcast.19), calls=%async_computation | async-start | bytes 2097152 | tf_op jit(solution)/shard_map/all_to_all | solution.py:407
  13.2 5.3 %copy-start.4 = (bf16[1,128,4,1024]{3,2,1,0:T(4,128)(2,1)S(1)}, bf16[1,128,4,1024]{3,2,1,0:T(4,128)(2,1)}, u32[]{:S(2)}) copy-start(bf16[1,128,4,1024]{3,2,1,0:T(4,128)(2,1)} %param.7) | copy-start | bytes 3145732
  13.2 5.7 %collective-permute-start = (s32[1,64]{1,0:T(1,128)S(1)}, s32[1,64]{1,0:T(1,128)S(1)}, u32[]{:S(2)}, u32[]{:S(2)}) collective-permute-start(s32[1,64]{1,0:T(1,128)S(1)} %copy-done.3), channel_id=1, source_target_pairs={{0,16},{16,0},{1,17},{17,1},{2,18},{18,2},{3,19},{19,3},{4,20},{20... | collective-permute-start | bytes 776 | tf_op jit(solution)/shard_map/ppermute | solution.py:360
  18.8 17.3 %copy-start.2 = (f32[8,128]{1,0:T(8,128)S(1)}, f32[8,128]{1,0:T(8,128)}, u32[]{:S(2)}) copy-start(f32[8,128]{1,0:T(8,128)} %get-tuple-element.14.refs_0_) | copy-start | bytes 12292
  40.1 31.7 %copy-start = (bf16[8,64,1024]{2,1,0:T(8,128)(2,1)S(1)}, bf16[8,64,1024]{2,1,0:T(8,128)(2,1)}, u32[]{:S(2)}) copy-start(bf16[8,64,1024]{2,1,0:T(8,128)(2,1)} %get-tuple-element.11.embedded) | copy-start | bytes 3145732
  40.1 31.7 %copy-start.1 = (bf16[8,8,64,128]{3,2,1,0:T(8,128)(2,1)S(1)}, bf16[8,8,64,128]{3,2,1,0:T(8,128)(2,1)}, u32[]{:S(2)}) copy-start(bf16[8,8,64,128]{3,2,1,0:T(8,128)(2,1)} %get-tuple-element.12.weights) | copy-start | bytes 3145732
  75.7 1.7 %collective-permute-start.1 = (bf16[32,1024]{1,0:T(8,128)(2,1)S(1)}, bf16[32,1024]{1,0:T(8,128)(2,1)S(1)}, u32[]{:S(2)}, u32[]{:S(2)}) collective-permute-start(bf16[32,1024]{1,0:T(8,128)(2,1)S(1)} %get-tuple-element.17), channel_id=1, source_target_pairs={{0,1},{1,0},{2,3},{3,2},{4,5},{5,4},{6,7},{7,6},{8,9},{9,8},{10,11... | collective-permute-start | bytes 196616 | tf_op jit(solution)/shard_map/ppermute | solution.py:444
  77.4 4.5 %collective-permute-start.2 = (bf16[32,1024]{1,0:T(8,128)(2,1)S(1)}, bf16[32,1024]{1,0:T(8,128)(2,1)S(1)}, u32[]{:S(2)}, u32[]{:S(2)}) collective-permute-start(bf16[32,1024]{1,0:T(8,128)(2,1)S(1)} %sums.3.refs_0_), channel_id=1, source_target_pairs={{0,4},{1,5},{2,6},{3,7},{4,0},{5,1},{6,2},{7,3},{8,12},{9,13},{10,... | collective-permute-start | bytes 196616 | tf_op jit(solution)/shard_map/ppermute | solution.py:444
  79.4 8.2 %collective-permute-start.3 = (bf16[32,1024]{1,0:T(8,128)(2,1)S(1)}, bf16[32,1024]{1,0:T(8,128)(2,1)S(1)}, u32[]{:S(2)}, u32[]{:S(2)}) collective-permute-start(bf16[32,1024]{1,0:T(8,128)(2,1)S(1)} %sums.3.refs_0_), channel_id=1, source_target_pairs={{0,8},{1,9},{2,10},{3,11},{4,12},{5,13},{6,14},{7,15},{8,0},{9,1},... | collective-permute-start | bytes 196616 | tf_op jit(solution)/shard_map/ppermute | solution.py:444
  80.3 7.3 %collective-permute-start.4 = (bf16[32,1024]{1,0:T(8,128)(2,1)S(1)}, bf16[32,1024]{1,0:T(8,128)(2,1)S(1)}, u32[]{:S(2)}, u32[]{:S(2)}) collective-permute-start(bf16[32,1024]{1,0:T(8,128)(2,1)S(1)} %sums.3.refs_0_), channel_id=1, source_target_pairs={{0,12},{1,13},{2,14},{3,15},{4,8},{5,9},{6,10},{7,11},{8,4},{9,5},... | collective-permute-start | bytes 196616 | tf_op jit(solution)/shard_map/ppermute | solution.py:444
  87.7 4.6 %collective-permute-start.5 = (bf16[32,1024]{1,0:T(8,128)(2,1)S(1)}, bf16[32,1024]{1,0:T(8,128)(2,1)S(1)}, u32[]{:S(2)}, u32[]{:S(2)}) collective-permute-start(bf16[32,1024]{1,0:T(8,128)(2,1)S(1)} %sums.4.refs_0_), channel_id=1, source_target_pairs={{0,2},{1,3},{2,0},{3,1},{4,6},{5,7},{6,4},{7,5},{8,10},{9,11},{10,... | collective-permute-start | bytes 196616 | tf_op jit(solution)/shard_map/ppermute | solution.py:444
  88.4 4.9 %collective-permute-start.6 = (bf16[32,1024]{1,0:T(8,128)(2,1)S(1)}, bf16[32,1024]{1,0:T(8,128)(2,1)S(1)}, u32[]{:S(2)}, u32[]{:S(2)}) collective-permute-start(bf16[32,1024]{1,0:T(8,128)(2,1)S(1)} %sums.4.refs_0_), channel_id=1, source_target_pairs={{0,16},{1,17},{2,18},{3,19},{4,20},{5,21},{6,22},{7,23},{8,24},{9,... | collective-permute-start | bytes 196616 | tf_op jit(solution)/shard_map/ppermute | solution.py:444
  89.9 5.2 %collective-permute-start.7 = (bf16[32,1024]{1,0:T(8,128)(2,1)S(1)}, bf16[32,1024]{1,0:T(8,128)(2,1)S(1)}, u32[]{:S(2)}, u32[]{:S(2)}) collective-permute-start(bf16[32,1024]{1,0:T(8,128)(2,1)S(1)} %sums.4.refs_0_), channel_id=1, source_target_pairs={{0,18},{1,19},{2,16},{3,17},{4,22},{5,23},{6,20},{7,21},{8,26},{9,... | collective-permute-start | bytes 196616 | tf_op jit(solution)/shard_map/ppermute | solution.py:444
  95.1 1.4 %collective-permute-start.8 = (bf16[2,32,1024]{2,1,0:T(8,128)(2,1)S(1)}, bf16[2,32,1024]{2,1,0:T(8,128)(2,1)S(1)}, u32[]{:S(2)}, u32[]{:S(2)}) collective-permute-start(bf16[2,32,1024]{2,1,0:T(8,128)(2,1)S(1)} %sums.5.refs_2_), channel_id=1, source_target_pairs={{0,1},{1,0},{2,3},{3,2},{4,5},{5,4},{6,7},{7,6},{8,9},{9,8},{10,11... | collective-permute-start | bytes 393224 | tf_op jit(solution)/shard_map/ppermute | solution.py:444

commit v3 on v2

--- a/solution.py
+++ b/solution.py
@@ -15,6 +15,8 @@
 SUBLANES = 8
 STEP = 512
 PIECES = 8
+PIECE = 256
+AHEAD = 2
 PLANE = 4
 SPATIAL_GROUP = 32
 TEMPORAL_GROUP = 8
@@ -159,31 +161,64 @@
 
 
 def spatial_kernel(
-    width, counts, offsets, layout, embedding, tokens, rows, mixed, spread, bias, by_electrode
+    width, counts, offsets, layout, all_embedding, all_tokens, all_rows, all_mixed,
+    spread, bias, by_electrode, embedding, tokens, rows, mixed, fetch_sems, write_sems,
 ):
-    patches, slots, model = tokens.shape
-    templates = embedding.shape[0]
+    pieces, patches, slots, model = tokens.shape
+    templates = embedding.shape[1]
     pairs = model // LANES
 
-    @pl.when(pl.program_id(0) == 0)
-    def _():
-        bias[...] = pair_bias(counts, offsets, slots)
-        wanted = jnp.broadcast_to(layout[...].astype(jnp.float32), (LANES, slots))
-        wanted = jnp.transpose(wanted).astype(jnp.int32)
-        template = lax.broadcasted_iota(jnp.int32, (slots, LANES), 1)
-        for first in range(0, templates, LANES):
-            chosen = wanted == template + first
-            spread[:, pl.ds(first, LANES)] = chosen.astype(jnp.float32).astype(jnp.bfloat16)
-
-    chosen_rows = dot(spread[...], embedding[...], (1, 0))
-    rows[...] = chosen_rows.astype(jnp.bfloat16)
-    for group in in_groups(pairs, patches, SPATIAL_GROUP):
-        values, shares = attention(width, tokens, chosen_rows, bias, group)
-        attended = by_query(shares, values, width)
-        for (pair, p), value, result in zip(group, values, attended):
-            by_electrode[pair, of_patch(p, slots, patches), :] = value.astype(jnp.float32) + result
-    for pair in range(pairs):
-        mixed[:, pair_columns(pair)] = by_electrode[pair].astype(jnp.bfloat16)
+    def fetches(at):
+        columns = pl.ds(at * model, model)
+        return (
+            pltpu.make_async_copy(
+                all_tokens.at[:, :, columns], tokens.at[at], fetch_sems.at[at, 0]
+            ),
+            pltpu.make_async_copy(
+                all_embedding.at[:, columns], embedding.at[at], fetch_sems.at[at, 1]
+            ),
+        )
+
+    def writes(at):
+        columns = pl.ds(at * model, model)
+        return (
+            pltpu.make_async_copy(rows.at[at], all_rows.at[:, columns], write_sems.at[at, 0]),
+            pltpu.make_async_copy(mixed.at[at], all_mixed.at[:, columns], write_sems.at[at, 1]),
+        )
+
+    for at in range(min(AHEAD, pieces)):
+        for copy in fetches(at):
+            copy.start()
+    bias[...] = pair_bias(counts, offsets, slots)
+    wanted = jnp.broadcast_to(layout[...].astype(jnp.float32), (LANES, slots))
+    wanted = jnp.transpose(wanted).astype(jnp.int32)
+    template = lax.broadcasted_iota(jnp.int32, (slots, LANES), 1)
+    for first in range(0, templates, LANES):
+        chosen = wanted == template + first
+        spread[:, pl.ds(first, LANES)] = chosen.astype(jnp.float32).astype(jnp.bfloat16)
+
+    for at in range(pieces):
+        for copy in fetches(at):
+            copy.wait()
+        if at + AHEAD < pieces:
+            for copy in fetches(at + AHEAD):
+                copy.start()
+        chosen_rows = dot(spread[...], embedding[at], (1, 0))
+        rows[at] = chosen_rows.astype(jnp.bfloat16)
+        for group in in_groups(pairs, patches, SPATIAL_GROUP):
+            values, shares = attention(width, tokens.at[at], chosen_rows, bias, group)
+            attended = by_query(shares, values, width)
+            for (pair, p), value, result in zip(group, values, attended):
+                by_electrode[at * pairs + pair, of_patch(p, slots, patches), :] = (
+                    value.astype(jnp.float32) + result
+                )
+        for pair in range(pairs):
+            mixed[at, :, pair_columns(pair)] = by_electrode[at * pairs + pair].astype(jnp.bfloat16)
+        for copy in writes(at):
+            copy.start()
+    for at in range(pieces):
+        for copy in writes(at):
+            copy.wait()
 
 
 def weights_kernel(width, counts, offsets, rows, tokens, embedded, weights, made, bias):
@@ -214,38 +249,49 @@
 
 
 def temporal_kernel(width, parts, mixed, out_grad, *refs):
-    mixed_grad, received, returned = refs[-3:]
+    all_mixed_grad, received, returned, mixed_grad, sems = refs[-5:]
     electrodes, patches, _ = out_grad.shape
-    model = mixed_grad.shape[1]
+    pieces, _, model = mixed_grad.shape
     local = patches // parts
     pairs = model // LANES
     score_masks = head_masks(width, 0.5 / math.sqrt(width))
     ones = head_masks(width, 1.0)
-    for pair in range(pairs):
-        received[pair] = mixed[:, step_columns(pair, model)].astype(jnp.float32)
-    for group in in_groups(pairs, electrodes, TEMPORAL_GROUP):
-        places = [electrode_rows(e, electrodes, parts, local) for _, e in group]
-        values = each(
-            lambda item, place: jnp.concatenate(
-                [received[item[0], rows, :] for rows in place], axis=0
-            ).astype(jnp.bfloat16),
-            group,
-            places,
+    copies = []
+    for at in range(pieces):
+        first = at * pairs
+        for pair in range(first, first + pairs):
+            received[pair] = mixed[:, pair_columns(pair)].astype(jnp.float32)
+        for group in in_groups(pairs, electrodes, TEMPORAL_GROUP):
+            group = [(first + pair, e) for pair, e in group]
+            places = [electrode_rows(e, electrodes, parts, local) for _, e in group]
+            values = each(
+                lambda item, place: jnp.concatenate(
+                    [received[item[0], rows, :] for rows in place], axis=0
+                ).astype(jnp.bfloat16),
+                group,
+                places,
+            )
+            cotangents = [out_grad[e, :, pair_columns(pair)] for pair, e in group]
+            scaled = each(lambda v: head_rows(v, score_masks), values)
+            scores = each(lambda v, s: dot(v, s, (1, 1)), values, scaled)
+            heads_grads = each(lambda g: head_rows(g, ones), cotangents)
+            grad_weights = each(lambda v, g: dot(v, g, (1, 1)), values, heads_grads)
+            shares = weights_by_key(scores)
+            grads = back(values, scaled, cotangents, shares, grad_weights, heads_grads, width)
+            for (pair, _), place, grad in zip(group, places, grads):
+                start = 0
+                for rows in place:
+                    returned[pair, rows, :] = grad[start : start + rows.size]
+                    start += rows.size
+        for pair in range(pairs):
+            mixed_grad[at, :, pair_columns(pair)] = returned[first + pair].astype(jnp.bfloat16)
+        copy = pltpu.make_async_copy(
+            mixed_grad.at[at], all_mixed_grad.at[:, pl.ds(at * model, model)], sems.at[at]
         )
-        cotangents = [out_grad[e, :, step_columns(pair, model)] for pair, e in group]
-        scaled = each(lambda v: head_rows(v, score_masks), values)
-        scores = each(lambda v, s: dot(v, s, (1, 1)), values, scaled)
-        heads_grads = each(lambda g: head_rows(g, ones), cotangents)
-        grad_weights = each(lambda v, g: dot(v, g, (1, 1)), values, heads_grads)
-        shares = weights_by_key(scores)
-        grads = back(values, scaled, cotangents, shares, grad_weights, heads_grads, width)
-        for (pair, _), place, grad in zip(group, places, grads):
-            start = 0
-            for rows in place:
-                returned[pair, rows, :] = grad[start : start + rows.size]
-                start += rows.size
-    for pair in range(pairs):
-        mixed_grad[:, pair_columns(pair)] = returned[pair].astype(jnp.bfloat16)
+        copy.start()
+        copies.append(copy)
+    for copy in copies:
+        copy.wait()
 
 
 def half_rows(bit, away, count):
@@ -372,16 +418,24 @@
     flat_scratch = pltpu.VMEM((pairs, slots * local, LANES), jnp.float32)
 
     strip = pl.BlockSpec((slots, STEP), lambda step: (0, step))
+    pieces = model // PIECE
+    all_pairs = pltpu.VMEM((model // LANES, slots * local, LANES), jnp.float32)
+    flat_pieces = pltpu.VMEM((pieces, slots * local, PIECE), jnp.bfloat16)
     rows, mixed = pl.pallas_call(
         functools.partial(spatial_kernel, width),
-        grid=(steps,),
         out_shape=(jax.ShapeDtypeStruct((slots, model), jnp.bfloat16), flat_shape),
-        in_specs=[SMEM, SMEM, VMEM, pl.BlockSpec((templates, STEP), lambda step: (0, step)), planes],
-        out_specs=(strip, flat),
+        in_specs=[SMEM, SMEM, VMEM, HBM, HBM],
+        out_specs=(HBM, HBM),
         scratch_shapes=[
             pltpu.VMEM((slots, templates), jnp.bfloat16),
             pltpu.VMEM((slots, 2 * slots), jnp.float32),
-            flat_scratch,
+            all_pairs,
+            pltpu.VMEM((pieces, templates, PIECE), jnp.bfloat16),
+            pltpu.VMEM((pieces, local, slots, PIECE), jnp.bfloat16),
+            pltpu.VMEM((pieces, slots, PIECE), jnp.bfloat16),
+            flat_pieces,
+            pltpu.SemaphoreType.DMA((pieces, 2)),
+            pltpu.SemaphoreType.DMA((pieces, 2)),
         ],
         compiler_params=STREAMED,
         name="spatial",
@@ -407,12 +461,10 @@
     gathered = lax.all_to_all(mixed, "shard", split_axis=0, concat_axis=0, tiled=True)
     mixed_grad = pl.pallas_call(
         functools.partial(temporal_kernel, width, parts),
-        grid=(steps,),
         out_shape=flat_shape,
-        in_specs=[VMEM, VMEM]
-        + [pl.BlockSpec(memory_space=pl.ANY)] * groups,
-        out_specs=flat,
-        scratch_shapes=[flat_scratch, flat_scratch],
+        in_specs=[VMEM, VMEM] + [pl.BlockSpec(memory_space=pl.ANY)] * groups,
+        out_specs=HBM,
+        scratch_shapes=[all_pairs, all_pairs, flat_pieces, pltpu.SemaphoreType.DMA((pieces,))],
         compiler_params=PARAMS,
         name="temporal",
     )(gathered, cotangent, made, *layouts[1:])

time: 98 us -> 100 us (1.020)
  Pallas kernels: 18.1 us -> 20.1 us
    pallas_call x2, Pallas kernels: 9.03 us -> 11.1 us  [the longest x1 6.4 us: body(): pl.pallas_call(functools.partial(spatial_kernel, width), out_shape=(jax.S...]
where the time goes in v3:
time: 100 us; the launch traced here: 99.7 us
  blocking collectives  31.6 us (32%)
  waiting for transfers between devices  29 us (29%)
  Pallas kernels  20.1 us (20%)
  starting transfers between devices  17.8 us (18%)
    all_to_all x1, blocking collectives, body(): lax.all_to_all(mixed_grad, 'shard', split_axis=0, concat_axis=0, tiled=True)  31.6 us
    all_to_all x1, waiting for transfers between devices, body(): lax.all_to_all(mixed, 'shard', split_axis=0, concat_axis=0, tiled=True)  17.3 us
    ppermute x8, waiting for transfers between devices, to_partner(): return lax.ppermute(array, ('group', 'shard'), pairs_of_devices)  11.8 us
    ppermute x8, starting transfers between devices, to_partner(): return lax.ppermute(array, ('group', 'shard'), pairs_of_devices)  8.85 us
    all_to_all x1, starting transfers between devices, body(): lax.all_to_all(mixed, 'shard', split_axis=0, concat_axis=0, tiled=True)  7.37 us
    pallas_call x1, Pallas kernels, body(): pl.pallas_call(functools.partial(spatial_kernel, width), out_shape=(jax.S...  6.4 us
    pallas_call x1, Pallas kernels, body(): pl.pallas_call(functools.partial(temporal_kernel, width, parts), out_shap...  4.66 us
    pallas_call x1, Pallas kernels, body(): pl.pallas_call(functools.partial(spatial_back_kernel, width), grid=(steps...  3.97 us
  transfers between devices with their start and end apart: 10, of which 8 were waited for; matrix products, arithmetic and copies ran while one was open for 0% of the time, Pallas kernels for 4%

profile of v3, /device:TPU:0, one launch (start us, length us, event | category | flops | bytes accessed | tf_op | source)
XLA Modules:
  0.0 99.7 jit_solution(13196741311874780776)
XLA Ops:
  0.6 6.4 %spatial.1 = (bf16[64,1024]{1,0:T(8,128)(2,1)}, bf16[512,1024]{1,0:T(8,128)(2,1)}) custom-call(s32[1,2]{1,0:T(1,128)} %counts.3, s32[1,2]{1,0:T(1,128)} %offsets.3, s32[1,64]{1,0:T(1,128)} %refs_0_.1, bf16[512,1024]{1,0:T(8,128)(2,1)} %all_embedding.1, bf16[8,64,1024]{2,1,0:T(8,128)(2,1)} %bitcast.16), custom_call_target="tpu_custom_call" | custom-call | tf_op jit(solution)/shard_map/spatial/pallas_call | solution.py:424
  7.0 7.4 %all-to-all-start = ((bf16[16,32,1024]{2,1,0:T(8,128)(2,1)}), bf16[16,32,1024]{2,1,0:T(8,128)(2,1)S(1)}, u32[]{:S(2)}, u32[]{:S(2)}) async-start(bf16[16,32,1024]{2,1,0:T(8,128)(2,1)} %bitcast.19), calls=%async_computation | async-start | bytes 2097152 | tf_op jit(solution)/shard_map/all_to_all | solution.py:461
  14.4 1.6 %collective-permute-start = (s32[1,64]{1,0:T(1,128)S(1)}, s32[1,64]{1,0:T(1,128)S(1)}, u32[]{:S(2)}, u32[]{:S(2)}) collective-permute-start(s32[1,64]{1,0:T(1,128)S(1)} %copy-done.3), channel_id=1, source_target_pairs={{0,16},{16,0},{1,17},{17,1},{2,18},{18,2},{3,19},{19,3},{4,20},{20... | collective-permute-start | bytes 776 | tf_op jit(solution)/shard_map/ppermute | solution.py:406
  16.0 3.7 %weights.1 = (bf16[8,64,1024]{2,1,0:T(8,128)(2,1)}, bf16[8,8,64,128]{3,2,1,0:T(8,128)(2,1)}, f32[8,128]{1,0:T(8,128)}) custom-call(s32[1,2]{1,0:T(1,128)} %counts.3, s32[1,2]{1,0:T(1,128)} %offsets.3, bf16[64,1024]{1,0:T(8,128)(2,1)} %get-tuple-element.10.rows, bf16[8,64,1024]{2,1,0:T(8,128)(2,1)} %bitcast.17), custom_call_target="tpu_custom_call" | custom-call | flops 134217728 | bytes 3145728 | tf_op jit(solution)/shard_map/weights/pallas_call | solution.py:443
  19.8 0.3 copy.10
  20.1 17.3 %all-to-all-done = bf16[16,32,1024]{2,1,0:T(8,128)(2,1)S(1)} async-done(((bf16[16,32,1024]{2,1,0:T(8,128)(2,1)}), bf16[16,32,1024]{2,1,0:T(8,128)(2,1)S(1)}, u32[]{:S(2)}, u32[]{:S(2)}) %all-to-all-start) | async-done | bytes 1048608 | tf_op jit(solution)/shard_map/all_to_all | solution.py:461
  37.4 4.7 %temporal.1 = bf16[512,1024]{1,0:T(8,128)(2,1)S(1)} custom-call(bf16[512,1024]{1,0:T(8,128)(2,1)S(1)} %bitcast.13, bf16[4,128,1024]{2,1,0:T(8,128)(2,1)S(1)} %bitcast.14, f32[8,128]{1,0:T(8,128)S(1)} %copy-done.2, s32[1,64]{1,0:T(1,128)S(1)} %collective-permute-done.refs_1_), custom_call_target="tpu_custom_call" | custom-call | tf_op jit(solution)/shard_map/temporal/pallas_call | solution.py:462
  42.1 31.6 %all_to_all.22 = bf16[16,32,1024]{2,1,0:T(8,128)(2,1)S(1)} all-to-all(bf16[16,32,1024]{2,1,0:T(8,128)(2,1)S(1)} %bitcast.15), channel_id=1, replica_groups=mesh['group'=2,'shard'=16] {'shard'}, dimensions={0} | all-to-all | bytes 2097152 | tf_op jit(solution)/shard_map/all_to_all | solution.py:472
  73.7 4.0 %spatial_back.1 = (bf16[8,64,1024]{2,1,0:T(8,128)(2,1)}, bf16[32,1024]{1,0:T(8,128)(2,1)S(1)}, bf16[32,1024]{1,0:T(8,128)(2,1)S(1)}) custom-call(bf16[8,64,1024]{2,1,0:T(8,128)(2,1)S(1)} %copy-done, bf16[8,8,64,128]{3,2,1,0:T(8,128)(2,1)S(1)} %copy-done.1, bf16[512,1024]{1,0:T(8,128)(2,1)S(1)} %bitcast.12), custom_call_target="tpu_custom_call" | custom-call | tf_op jit(solution)/shard_map/spatial_back/pallas_call | solution.py:474
  77.7 0.8 collective-permute-start.1
  78.5 0.9 collective-permute-done.1.arrived
  79.4 1.9 %collective-permute-start.2 = (bf16[32,1024]{1,0:T(8,128)(2,1)S(1)}, bf16[32,1024]{1,0:T(8,128)(2,1)S(1)}, u32[]{:S(2)}, u32[]{:S(2)}) collective-permute-start(bf16[32,1024]{1,0:T(8,128)(2,1)S(1)} %sums.3.refs_0_), channel_id=1, source_target_pairs={{0,4},{1,5},{2,6},{3,7},{4,0},{5,1},{6,2},{7,3},{8,12},{9,13},{10,... | collective-permute-start | bytes 196616 | tf_op jit(solution)/shard_map/ppermute | solution.py:496
  81.3 0.9 collective-permute-start.3
  82.2 1.6 %collective-permute-start.4 = (bf16[32,1024]{1,0:T(8,128)(2,1)S(1)}, bf16[32,1024]{1,0:T(8,128)(2,1)S(1)}, u32[]{:S(2)}, u32[]{:S(2)}) collective-permute-start(bf16[32,1024]{1,0:T(8,128)(2,1)S(1)} %sums.3.refs_0_), channel_id=1, source_target_pairs={{0,12},{1,13},{2,14},{3,15},{4,8},{5,9},{6,10},{7,11},{8,4},{9,5},... | collective-permute-start | bytes 196616 | tf_op jit(solution)/shard_map/ppermute | solution.py:496
  83.9 5.6 %collective-permute-done.3.refs_2_ = bf16[32,1024]{1,0:T(8,128)(2,1)S(1)} collective-permute-done((bf16[32,1024]{1,0:T(8,128)(2,1)S(1)}, bf16[32,1024]{1,0:T(8,128)(2,1)S(1)}, u32[]{:S(2)}, u32[]{:S(2)}) %collective-permute-start.3) | collective-permute-done | bytes 65568 | tf_op jit(solution)/shard_map/ppermute | solution.py:496
  89.6 0.7 collective-permute-start.5
  90.3 1.5 %collective-permute-start.6 = (bf16[32,1024]{1,0:T(8,128)(2,1)S(1)}, bf16[32,1024]{1,0:T(8,128)(2,1)S(1)}, u32[]{:S(2)}, u32[]{:S(2)}) collective-permute-start(bf16[32,1024]{1,0:T(8,128)(2,1)S(1)} %sums.4.refs_0_), channel_id=1, source_target_pairs={{0,16},{1,17},{2,18},{3,19},{4,20},{5,21},{6,22},{7,23},{8,24},{9,... | collective-permute-start | bytes 196616 | tf_op jit(solution)/shard_map/ppermute | solution.py:496
  91.8 1.4 %collective-permute-start.7 = (bf16[32,1024]{1,0:T(8,128)(2,1)S(1)}, bf16[32,1024]{1,0:T(8,128)(2,1)S(1)}, u32[]{:S(2)}, u32[]{:S(2)}) collective-permute-start(bf16[32,1024]{1,0:T(8,128)(2,1)S(1)} %sums.4.refs_0_), channel_id=1, source_target_pairs={{0,18},{1,19},{2,16},{3,17},{4,22},{5,23},{6,20},{7,21},{8,26},{9,... | collective-permute-start | bytes 196616 | tf_op jit(solution)/shard_map/ppermute | solution.py:496
  93.2 1.1 %collective-permute-done.5.refs_1_ = bf16[32,1024]{1,0:T(8,128)(2,1)S(1)} collective-permute-done((bf16[32,1024]{1,0:T(8,128)(2,1)S(1)}, bf16[32,1024]{1,0:T(8,128)(2,1)S(1)}, u32[]{:S(2)}, u32[]{:S(2)}) %collective-permute-start.5) | collective-permute-done | bytes 65568 | tf_op jit(solution)/shard_map/ppermute | solution.py:496
  94.2 1.0 collective-permute-done.6.refs_2_
  95.2 1.8 %collective-permute-done.7.refs_3_ = bf16[32,1024]{1,0:T(8,128)(2,1)S(1)} collective-permute-done((bf16[32,1024]{1,0:T(8,128)(2,1)S(1)}, bf16[32,1024]{1,0:T(8,128)(2,1)S(1)}, u32[]{:S(2)}, u32[]{:S(2)}) %collective-permute-start.7) | collective-permute-done | bytes 65568 | tf_op jit(solution)/shard_map/ppermute | solution.py:496
  97.0 0.1 collective-permute-start.8
  97.1 1.3 %collective-permute-done.8.refs_3_ = bf16[2,32,1024]{2,1,0:T(8,128)(2,1)S(1)} collective-permute-done((bf16[2,32,1024]{2,1,0:T(8,128)(2,1)S(1)}, bf16[2,32,1024]{2,1,0:T(8,128)(2,1)S(1)}, u32[]{:S(2)}, u32[]{:S(2)}) %collective-permute-start.8) | collective-permute-done | bytes 131104 | tf_op jit(solution)/shard_map/ppermute | solution.py:496
  98.4 1.2 %table.1 = f32[256,1024]{1,0:T(8,128)} custom-call(s32[1,64]{1,0:T(1,128)S(1)} %copy-done.3, s32[1,64]{1,0:T(1,128)S(1)} %collective-permute-done.refs_1_, bf16[2,32,1024]{2,1,0:T(8,128)(2,1)S(1)} %sums.5.refs_2_, bf16[2,32,1024]{2,1,0:T(8,128)(2,1)S(1)} %collective-permute-done.8.refs_3_), custom_call_target="tpu_custom_call" | custom-call | tf_op jit(solution)/shard_map/table/pallas_call | solution.py:521
  (16 shorter events, 0.2 us)
Async XLA Ops:
  7.0 7.4 %copy-start.3 = (s32[1,64]{1,0:T(1,128)S(1)}, s32[1,64]{1,0:T(1,128)}, u32[]{:S(2)}) copy-start(s32[1,64]{1,0:T(1,128)} %refs_0_.1) | copy-start | bytes 772
  7.0 30.3 %all-to-all-start = ((bf16[16,32,1024]{2,1,0:T(8,128)(2,1)}), bf16[16,32,1024]{2,1,0:T(8,128)(2,1)S(1)}, u32[]{:S(2)}, u32[]{:S(2)}) async-start(bf16[16,32,1024]{2,1,0:T(8,128)(2,1)} %bitcast.19), calls=%async_computation | async-start | bytes 2097152 | tf_op jit(solution)/shard_map/all_to_all | solution.py:461
  14.4 5.3 %copy-start.4 = (bf16[1,128,4,1024]{3,2,1,0:T(4,128)(2,1)S(1)}, bf16[1,128,4,1024]{3,2,1,0:T(4,128)(2,1)}, u32[]{:S(2)}) copy-start(bf16[1,128,4,1024]{3,2,1,0:T(4,128)(2,1)} %param.7) | copy-start | bytes 3145732
  14.4 5.7 %collective-permute-start = (s32[1,64]{1,0:T(1,128)S(1)}, s32[1,64]{1,0:T(1,128)S(1)}, u32[]{:S(2)}, u32[]{:S(2)}) collective-permute-start(s32[1,64]{1,0:T(1,128)S(1)} %copy-done.3), channel_id=1, source_target_pairs={{0,16},{16,0},{1,17},{17,1},{2,18},{18,2},{3,19},{19,3},{4,20},{20... | collective-permute-start | bytes 776 | tf_op jit(solution)/shard_map/ppermute | solution.py:406
  20.1 17.3 %copy-start.2 = (f32[8,128]{1,0:T(8,128)S(1)}, f32[8,128]{1,0:T(8,128)}, u32[]{:S(2)}) copy-start(f32[8,128]{1,0:T(8,128)} %get-tuple-element.14.refs_0_) | copy-start | bytes 12292
  42.0 31.7 %copy-start = (bf16[8,64,1024]{2,1,0:T(8,128)(2,1)S(1)}, bf16[8,64,1024]{2,1,0:T(8,128)(2,1)}, u32[]{:S(2)}) copy-start(bf16[8,64,1024]{2,1,0:T(8,128)(2,1)} %get-tuple-element.11.embedded) | copy-start | bytes 3145732
  42.1 31.7 %copy-start.1 = (bf16[8,8,64,128]{3,2,1,0:T(8,128)(2,1)S(1)}, bf16[8,8,64,128]{3,2,1,0:T(8,128)(2,1)}, u32[]{:S(2)}) copy-start(bf16[8,8,64,128]{3,2,1,0:T(8,128)(2,1)} %get-tuple-element.12.weights) | copy-start | bytes 3145732
  77.7 1.7 %collective-permute-start.1 = (bf16[32,1024]{1,0:T(8,128)(2,1)S(1)}, bf16[32,1024]{1,0:T(8,128)(2,1)S(1)}, u32[]{:S(2)}, u32[]{:S(2)}) collective-permute-start(bf16[32,1024]{1,0:T(8,128)(2,1)S(1)} %get-tuple-element.17), channel_id=1, source_target_pairs={{0,1},{1,0},{2,3},{3,2},{4,5},{5,4},{6,7},{7,6},{8,9},{9,8},{10,11... | collective-permute-start | bytes 196616 | tf_op jit(solution)/shard_map/ppermute | solution.py:496
  79.4 4.5 %collective-permute-start.2 = (bf16[32,1024]{1,0:T(8,128)(2,1)S(1)}, bf16[32,1024]{1,0:T(8,128)(2,1)S(1)}, u32[]{:S(2)}, u32[]{:S(2)}) collective-permute-start(bf16[32,1024]{1,0:T(8,128)(2,1)S(1)} %sums.3.refs_0_), channel_id=1, source_target_pairs={{0,4},{1,5},{2,6},{3,7},{4,0},{5,1},{6,2},{7,3},{8,12},{9,13},{10,... | collective-permute-start | bytes 196616 | tf_op jit(solution)/shard_map/ppermute | solution.py:496
  81.3 8.2 %collective-permute-start.3 = (bf16[32,1024]{1,0:T(8,128)(2,1)S(1)}, bf16[32,1024]{1,0:T(8,128)(2,1)S(1)}, u32[]{:S(2)}, u32[]{:S(2)}) collective-permute-start(bf16[32,1024]{1,0:T(8,128)(2,1)S(1)} %sums.3.refs_0_), channel_id=1, source_target_pairs={{0,8},{1,9},{2,10},{3,11},{4,12},{5,13},{6,14},{7,15},{8,0},{9,1},... | collective-permute-start | bytes 196616 | tf_op jit(solution)/shard_map/ppermute | solution.py:496
  82.2 7.3 %collective-permute-start.4 = (bf16[32,1024]{1,0:T(8,128)(2,1)S(1)}, bf16[32,1024]{1,0:T(8,128)(2,1)S(1)}, u32[]{:S(2)}, u32[]{:S(2)}) collective-permute-start(bf16[32,1024]{1,0:T(8,128)(2,1)S(1)} %sums.3.refs_0_), channel_id=1, source_target_pairs={{0,12},{1,13},{2,14},{3,15},{4,8},{5,9},{6,10},{7,11},{8,4},{9,5},... | collective-permute-start | bytes 196616 | tf_op jit(solution)/shard_map/ppermute | solution.py:496
  89.6 4.6 %collective-permute-start.5 = (bf16[32,1024]{1,0:T(8,128)(2,1)S(1)}, bf16[32,1024]{1,0:T(8,128)(2,1)S(1)}, u32[]{:S(2)}, u32[]{:S(2)}) collective-permute-start(bf16[32,1024]{1,0:T(8,128)(2,1)S(1)} %sums.4.refs_0_), channel_id=1, source_target_pairs={{0,2},{1,3},{2,0},{3,1},{4,6},{5,7},{6,4},{7,5},{8,10},{9,11},{10,... | collective-permute-start | bytes 196616 | tf_op jit(solution)/shard_map/ppermute | solution.py:496
  90.3 4.9 %collective-permute-start.6 = (bf16[32,1024]{1,0:T(8,128)(2,1)S(1)}, bf16[32,1024]{1,0:T(8,128)(2,1)S(1)}, u32[]{:S(2)}, u32[]{:S(2)}) collective-permute-start(bf16[32,1024]{1,0:T(8,128)(2,1)S(1)} %sums.4.refs_0_), channel_id=1, source_target_pairs={{0,16},{1,17},{2,18},{3,19},{4,20},{5,21},{6,22},{7,23},{8,24},{9,... | collective-permute-start | bytes 196616 | tf_op jit(solution)/shard_map/ppermute | solution.py:496
  91.8 5.2 %collective-permute-start.7 = (bf16[32,1024]{1,0:T(8,128)(2,1)S(1)}, bf16[32,1024]{1,0:T(8,128)(2,1)S(1)}, u32[]{:S(2)}, u32[]{:S(2)}) collective-permute-start(bf16[32,1024]{1,0:T(8,128)(2,1)S(1)} %sums.4.refs_0_), channel_id=1, source_target_pairs={{0,18},{1,19},{2,16},{3,17},{4,22},{5,23},{6,20},{7,21},{8,26},{9,... | collective-permute-start | bytes 196616 | tf_op jit(solution)/shard_map/ppermute | solution.py:496
  97.0 1.4 %collective-permute-start.8 = (bf16[2,32,1024]{2,1,0:T(8,128)(2,1)S(1)}, bf16[2,32,1024]{2,1,0:T(8,128)(2,1)S(1)}, u32[]{:S(2)}, u32[]{:S(2)}) collective-permute-start(bf16[2,32,1024]{2,1,0:T(8,128)(2,1)S(1)} %sums.5.refs_2_), channel_id=1, source_target_pairs={{0,1},{1,0},{2,3},{3,2},{4,5},{5,4},{6,7},{7,6},{8,9},{9,8},{10,11... | collective-permute-start | bytes 393224 | tf_op jit(solution)/shard_map/ppermute | solution.py:496

commit v4 on v2

--- a/solution.py
+++ b/solution.py
@@ -15,6 +15,7 @@
 SUBLANES = 8
 STEP = 512
 PIECES = 8
+PIECE = 256
 PLANE = 4
 SPATIAL_GROUP = 32
 TEMPORAL_GROUP = 8
@@ -145,11 +146,16 @@
     return pl.ds(patch, slots, stride=patches)
 
 
+def of_halves(halves, index):
+    count = halves[0].shape[0]
+    return halves[index // count].at[index % count]
+
+
 def attention(width, tokens, rows, bias, group):
     score_masks = head_masks(width, 0.5 / math.sqrt(width))
     values = [
         (
-            tokens[p, :, pair_columns(pair)].astype(jnp.float32)
+            of_halves(tokens, p)[:, pair_columns(pair)].astype(jnp.float32)
             + rows[:, pair * LANES : (pair + 1) * LANES]
         ).astype(jnp.bfloat16)
         for pair, p in group
@@ -159,10 +165,12 @@
 
 
 def spatial_kernel(
-    width, counts, offsets, layout, embedding, tokens, rows, mixed, spread, bias, by_electrode
+    width, counts, offsets, layout, embedding, other_embedding, tokens, other_tokens,
+    rows, mixed, spread, bias, by_electrode,
 ):
-    patches, slots, model = tokens.shape
-    templates = embedding.shape[0]
+    half, slots, model = tokens.shape
+    patches, tokens = 2 * half, (tokens, other_tokens)
+    templates = 2 * embedding.shape[0]
     pairs = model // LANES
 
     @pl.when(pl.program_id(0) == 0)
@@ -175,7 +183,8 @@
             chosen = wanted == template + first
             spread[:, pl.ds(first, LANES)] = chosen.astype(jnp.float32).astype(jnp.bfloat16)
 
-    chosen_rows = dot(spread[...], embedding[...], (1, 0))
+    chosen_rows = dot(spread[:, : templates // 2], embedding[...], (1, 0))
+    chosen_rows = chosen_rows + dot(spread[:, templates // 2 :], other_embedding[...], (1, 0))
     rows[...] = chosen_rows.astype(jnp.bfloat16)
     for group in in_groups(pairs, patches, SPATIAL_GROUP):
         values, shares = attention(width, tokens, chosen_rows, bias, group)
@@ -189,6 +198,7 @@
 def weights_kernel(width, counts, offsets, rows, tokens, embedded, weights, made, bias):
     made[...] = jnp.zeros_like(made)
     patches, slots, model = tokens.shape
+    tokens = (tokens,)
 
     @pl.when(pl.program_id(0) == 0)
     def _():
@@ -214,38 +224,50 @@
 
 
 def temporal_kernel(width, parts, mixed, out_grad, *refs):
-    mixed_grad, received, returned = refs[-3:]
+    all_mixed_grad, received, returned, mixed_grad, sems = refs[-5:]
     electrodes, patches, _ = out_grad.shape
-    model = mixed_grad.shape[1]
+    pieces, _, model = mixed_grad.shape
     local = patches // parts
     pairs = model // LANES
     score_masks = head_masks(width, 0.5 / math.sqrt(width))
     ones = head_masks(width, 1.0)
-    for pair in range(pairs):
-        received[pair] = mixed[:, step_columns(pair, model)].astype(jnp.float32)
-    for group in in_groups(pairs, electrodes, TEMPORAL_GROUP):
-        places = [electrode_rows(e, electrodes, parts, local) for _, e in group]
-        values = each(
-            lambda item, place: jnp.concatenate(
-                [received[item[0], rows, :] for rows in place], axis=0
-            ).astype(jnp.bfloat16),
-            group,
-            places,
+    copies = []
+    for at in range(pieces):
+        first = at * pairs
+        for pair in range(first, first + pairs):
+            received[pair] = mixed[:, pair_columns(pair)].astype(jnp.float32)
+        for group in in_groups(pairs, electrodes, TEMPORAL_GROUP):
+            group = [(first + pair, e) for pair, e in group]
+            places = [electrode_rows(e, electrodes, parts, local) for _, e in group]
+            values = each(
+                lambda item, place: jnp.concatenate(
+                    [received[item[0], rows, :] for rows in place], axis=0
+                ).astype(jnp.bfloat16),
+                group,
+                places,
+            )
+            cotangents = [out_grad[e, :, pair_columns(pair)] for pair, e in group]
+            scaled = each(lambda v: head_rows(v, score_masks), values)
+            scores = each(lambda v, s: dot(v, s, (1, 1)), values, scaled)
+            heads_grads = each(lambda g: head_rows(g, ones), cotangents)
+            grad_weights = each(lambda v, g: dot(v, g, (1, 1)), values, heads_grads)
+            shares = weights_by_key(scores)
+            grads = back(values, scaled, cotangents, shares, grad_weights, heads_grads, width)
+            for (pair, _), place, grad in zip(group, places, grads):
+                start = 0
+                for rows in place:
+                    returned[pair, rows, :] = grad[start : start + rows.size]
+                    start += rows.size
+        for pair in range(pairs):
+            mixed_grad[at, :, pair_columns(pair)] = returned[first + pair].astype(jnp.bfloat16)
+    for at in range(pieces):
+        copy = pltpu.make_async_copy(
+            mixed_grad.at[at], all_mixed_grad.at[:, pl.ds(at * model, model)], sems.at[at]
         )
-        cotangents = [out_grad[e, :, step_columns(pair, model)] for pair, e in group]
-        scaled = each(lambda v: head_rows(v, score_masks), values)
-        scores = each(lambda v, s: dot(v, s, (1, 1)), values, scaled)
-        heads_grads = each(lambda g: head_rows(g, ones), cotangents)
-        grad_weights = each(lambda v, g: dot(v, g, (1, 1)), values, heads_grads)
-        shares = weights_by_key(scores)
-        grads = back(values, scaled, cotangents, shares, grad_weights, heads_grads, width)
-        for (pair, _), place, grad in zip(group, places, grads):
-            start = 0
-            for rows in place:
-                returned[pair, rows, :] = grad[start : start + rows.size]
-                start += rows.size
-    for pair in range(pairs):
-        mixed_grad[:, pair_columns(pair)] = returned[pair].astype(jnp.bfloat16)
+        copy.start()
+        copies.append(copy)
+    for copy in copies:
+        copy.wait()
 
 
 def half_rows(bit, away, count):
@@ -253,9 +275,12 @@
     return pl.ds(pl.multiple_of(lax.bitwise_xor(here, away) * count, count), count)
 
 
-def spatial_back_kernel(width, embedded, weights, mixed_grad, input_grad, *refs):
+def spatial_back_kernel(
+    width, embedded, other_embedded, weights, other_weights, mixed_grad, input_grad, *refs
+):
     electrode_grads, (sums, received) = refs[:-2], refs[-2:]
-    patches, slots, model = embedded.shape
+    patches, slots, model = input_grad.shape
+    embedded, weights = (embedded, other_embedded), (weights, other_weights)
     pairs = model // LANES
     score_masks = head_masks(width, 0.5 / math.sqrt(width))
     ones = head_masks(width, 1.0)
@@ -267,8 +292,8 @@
             received[pair, of_patch(p, slots, patches), :].astype(jnp.bfloat16)
             for pair, p in group
         ]
-        values = [embedded[p, :, pair_columns(pair)] for pair, p in group]
-        shares = [weights[p, pair] for pair, p in group]
+        values = [of_halves(embedded, p)[:, pair_columns(pair)] for pair, p in group]
+        shares = [of_halves(weights, p)[pair] for pair, p in group]
         scaled = each(lambda v: head_rows(v, score_masks), values)
         heads_grads = each(lambda g: head_rows(g, ones), cotangents)
         grad_weights = each(lambda v, g: dot(v, g, (1, 1)), values, heads_grads)
@@ -372,11 +397,30 @@
     flat_scratch = pltpu.VMEM((pairs, slots * local, LANES), jnp.float32)
 
     strip = pl.BlockSpec((slots, STEP), lambda step: (0, step))
+    pieces = model // PIECE
+    all_pairs = pltpu.VMEM((model // LANES, slots * local, LANES), jnp.float32)
+    flat_pieces = pltpu.VMEM((pieces, slots * local, PIECE), jnp.bfloat16)
+
+    def halves_of(shape, axis):
+        cut = tuple(size // 2 if place == axis else size for place, size in enumerate(shape[1]))
+        return [
+            pl.BlockSpec(
+                cut,
+                lambda step, half=half: tuple(
+                    half if place == axis else step if place == shape[0] else 0
+                    for place in range(len(cut))
+                ),
+            )
+            for half in range(2)
+        ]
+
     rows, mixed = pl.pallas_call(
         functools.partial(spatial_kernel, width),
         grid=(steps,),
         out_shape=(jax.ShapeDtypeStruct((slots, model), jnp.bfloat16), flat_shape),
-        in_specs=[SMEM, SMEM, VMEM, pl.BlockSpec((templates, STEP), lambda step: (0, step)), planes],
+        in_specs=[SMEM, SMEM, VMEM]
+        + halves_of((1, (templates, STEP)), 0)
+        + halves_of((2, (local, slots, STEP)), 0),
         out_specs=(strip, flat),
         scratch_shapes=[
             pltpu.VMEM((slots, templates), jnp.bfloat16),
@@ -385,7 +429,7 @@
         ],
         compiler_params=STREAMED,
         name="spatial",
-    )(counts, offsets, layout, embedding, tokens)
+    )(counts, offsets, layout, embedding, embedding, tokens, tokens)
     embedded, weights, made = pl.pallas_call(
         functools.partial(weights_kernel, width),
         grid=(steps,),
@@ -407,12 +451,10 @@
     gathered = lax.all_to_all(mixed, "shard", split_axis=0, concat_axis=0, tiled=True)
     mixed_grad = pl.pallas_call(
         functools.partial(temporal_kernel, width, parts),
-        grid=(steps,),
         out_shape=flat_shape,
-        in_specs=[VMEM, VMEM]
-        + [pl.BlockSpec(memory_space=pl.ANY)] * groups,
-        out_specs=flat,
-        scratch_shapes=[flat_scratch, flat_scratch],
+        in_specs=[VMEM, VMEM] + [pl.BlockSpec(memory_space=pl.ANY)] * groups,
+        out_specs=HBM,
+        scratch_shapes=[all_pairs, all_pairs, flat_pieces, pltpu.SemaphoreType.DMA((pieces,))],
         compiler_params=PARAMS,
         name="temporal",
     )(gathered, cotangent, made, *layouts[1:])
@@ -423,12 +465,14 @@
         functools.partial(spatial_back_kernel, width),
         grid=(steps,),
         out_shape=(plane_shape,) + (jax.ShapeDtypeStruct((half, model), jnp.bfloat16),) * 2,
-        in_specs=[planes, squares, VMEM],
+        in_specs=halves_of((2, (local, slots, STEP)), 0)
+        + halves_of((1, (local, pairs, slots, 2 * slots)), 0)
+        + [VMEM],
         out_specs=(planes,) + (pl.BlockSpec((half, STEP), lambda step: (0, step)),) * 2,
         scratch_shapes=[pltpu.VMEM((pairs, slots, LANES), jnp.float32), flat_scratch],
         compiler_params=PARAMS,
         name="spatial_back",
-    )(embedded, weights, returned)
+    )(embedded, embedded, weights, weights, returned)
 
     far_count = parts // PLANE
     assert parts == far_count * PLANE and parts & (parts - 1) == 0

time: 98 us -> 97.8 us (level)
  no operation moved by 1% of the time
where the time goes in v4:
time: 97.8 us; the launch traced here: 97.5 us
  blocking collectives  31.6 us (32%)
  waiting for transfers between devices  29 us (30%)
  Pallas kernels  18 us (18%)
  starting transfers between devices  17.8 us (18%)
    all_to_all x1, blocking collectives, body(): lax.all_to_all(mixed_grad, 'shard', split_axis=0, concat_axis=0, tiled=True)  31.6 us
    all_to_all x1, waiting for transfers between devices, body(): lax.all_to_all(mixed, 'shard', split_axis=0, concat_axis=0, tiled=True)  17.3 us
    ppermute x8, waiting for transfers between devices, to_partner(): return lax.ppermute(array, ('group', 'shard'), pairs_of_devices)  11.7 us
    ppermute x8, starting transfers between devices, to_partner(): return lax.ppermute(array, ('group', 'shard'), pairs_of_devices)  8.85 us
    all_to_all x1, starting transfers between devices, body(): lax.all_to_all(mixed, 'shard', split_axis=0, concat_axis=0, tiled=True)  7.36 us
    pallas_call x1, Pallas kernels, body(): pl.pallas_call(functools.partial(spatial_kernel, width), grid=(steps,), o...  5.04 us
    pallas_call x1, Pallas kernels, body(): pl.pallas_call(functools.partial(spatial_back_kernel, width), grid=(steps...  3.98 us
    pallas_call x1, Pallas kernels, body(): pl.pallas_call(functools.partial(temporal_kernel, width, parts), out_shap...  3.86 us
  transfers between devices with their start and end apart: 10, of which 8 were waited for; matrix products, arithmetic and copies ran while one was open for 0% of the time, Pallas kernels for 4%

profile of v4, /device:TPU:0, one launch (start us, length us, event | category | flops | bytes accessed | tf_op | source)
XLA Modules:
  0.0 97.5 jit_solution(4506699973290974073)
XLA Ops:
  0.6 5.0 %spatial.1 = (bf16[64,1024]{1,0:T(8,128)(2,1)}, bf16[512,1024]{1,0:T(8,128)(2,1)}) custom-call(s32[1,2]{1,0:T(1,128)} %counts.3, s32[1,2]{1,0:T(1,128)} %offsets.3, s32[1,64]{1,0:T(1,128)} %refs_0_.1, bf16[512,1024]{1,0:T(8,128)(2,1)} %other_embedding.1, bf16[512,1024]{1,0:T(8,128)(2,1)} %other_embedding.1, bf16[8,64,1024]{2,1,0:T(8,128)(2,1)} %bitcast.16, ...), custom_call_target="tpu_custom_call" | custom-call | tf_op jit(solution)/shard_map/spatial/pallas_call | solution.py:417
  5.7 7.4 %all-to-all-start = ((bf16[16,32,1024]{2,1,0:T(8,128)(2,1)}), bf16[16,32,1024]{2,1,0:T(8,128)(2,1)S(1)}, u32[]{:S(2)}, u32[]{:S(2)}) async-start(bf16[16,32,1024]{2,1,0:T(8,128)(2,1)} %bitcast.20), calls=%async_computation | async-start | bytes 2097152 | tf_op jit(solution)/shard_map/all_to_all | solution.py:451
  13.1 1.6 %collective-permute-start = (s32[1,64]{1,0:T(1,128)S(1)}, s32[1,64]{1,0:T(1,128)S(1)}, u32[]{:S(2)}, u32[]{:S(2)}) collective-permute-start(s32[1,64]{1,0:T(1,128)S(1)} %copy-done.3), channel_id=1, source_target_pairs={{0,16},{16,0},{1,17},{17,1},{2,18},{18,2},{3,19},{19,3},{4,20},{20... | collective-permute-start | bytes 776 | tf_op jit(solution)/shard_map/ppermute | solution.py:385
  14.7 3.7 %weights.1 = (bf16[8,64,1024]{2,1,0:T(8,128)(2,1)}, bf16[8,8,64,128]{3,2,1,0:T(8,128)(2,1)}, f32[8,128]{1,0:T(8,128)}) custom-call(s32[1,2]{1,0:T(1,128)} %counts.3, s32[1,2]{1,0:T(1,128)} %offsets.3, bf16[64,1024]{1,0:T(8,128)(2,1)} %get-tuple-element.10.rows, bf16[8,64,1024]{2,1,0:T(8,128)(2,1)} %bitcast.18), custom_call_target="tpu_custom_call" | custom-call | flops 134217728 | bytes 3145728 | tf_op jit(solution)/shard_map/weights/pallas_call | solution.py:433
  18.4 0.3 copy.10
  18.7 17.3 %all-to-all-done = bf16[16,32,1024]{2,1,0:T(8,128)(2,1)S(1)} async-done(((bf16[16,32,1024]{2,1,0:T(8,128)(2,1)}), bf16[16,32,1024]{2,1,0:T(8,128)(2,1)S(1)}, u32[]{:S(2)}, u32[]{:S(2)}) %all-to-all-start) | async-done | bytes 1048608 | tf_op jit(solution)/shard_map/all_to_all | solution.py:451
  36.0 3.9 %temporal.1 = bf16[512,1024]{1,0:T(8,128)(2,1)S(1)} custom-call(bf16[512,1024]{1,0:T(8,128)(2,1)S(1)} %bitcast.13, bf16[4,128,1024]{2,1,0:T(8,128)(2,1)S(1)} %bitcast.14, f32[8,128]{1,0:T(8,128)S(1)} %copy-done.2, s32[1,64]{1,0:T(1,128)S(1)} %collective-permute-done.refs_1_), custom_call_target="tpu_custom_call" | custom-call | tf_op jit(solution)/shard_map/temporal/pallas_call | solution.py:452
  39.9 31.6 %all_to_all.22 = bf16[16,32,1024]{2,1,0:T(8,128)(2,1)S(1)} all-to-all(bf16[16,32,1024]{2,1,0:T(8,128)(2,1)S(1)} %bitcast.15), channel_id=1, replica_groups=mesh['group'=2,'shard'=16] {'shard'}, dimensions={0} | all-to-all | bytes 2097152 | tf_op jit(solution)/shard_map/all_to_all | solution.py:462
  71.5 4.0 %spatial_back.1 = (bf16[8,64,1024]{2,1,0:T(8,128)(2,1)}, bf16[32,1024]{1,0:T(8,128)(2,1)S(1)}, bf16[32,1024]{1,0:T(8,128)(2,1)S(1)}) custom-call(bf16[8,64,1024]{2,1,0:T(8,128)(2,1)S(1)} %copy-done, bf16[8,64,1024]{2,1,0:T(8,128)(2,1)S(1)} %copy-done, bf16[8,8,64,128]{3,2,1,0:T(8,128)(2,1)S(1)} %copy-done.1, bf16[8,8,64,128]{3,2,1,0:T(8,128)(2,1)S(1)} %copy-done.1, ...), custom_call_target="tpu_custom_call" | custom-call | tf_op jit(solution)/shard_map/spatial_back/pallas_call | solution.py:464
  75.5 0.8 collective-permute-start.1
  76.3 0.9 collective-permute-done.1.arrived
  77.2 1.9 %collective-permute-start.2 = (bf16[32,1024]{1,0:T(8,128)(2,1)S(1)}, bf16[32,1024]{1,0:T(8,128)(2,1)S(1)}, u32[]{:S(2)}, u32[]{:S(2)}) collective-permute-start(bf16[32,1024]{1,0:T(8,128)(2,1)S(1)} %sums.3.refs_0_), channel_id=1, source_target_pairs={{0,4},{1,5},{2,6},{3,7},{4,0},{5,1},{6,2},{7,3},{8,12},{9,13},{10,... | collective-permute-start | bytes 196616 | tf_op jit(solution)/shard_map/ppermute | solution.py:488
  79.1 0.9 collective-permute-start.3
  80.0 1.6 %collective-permute-start.4 = (bf16[32,1024]{1,0:T(8,128)(2,1)S(1)}, bf16[32,1024]{1,0:T(8,128)(2,1)S(1)}, u32[]{:S(2)}, u32[]{:S(2)}) collective-permute-start(bf16[32,1024]{1,0:T(8,128)(2,1)S(1)} %sums.3.refs_0_), channel_id=1, source_target_pairs={{0,12},{1,13},{2,14},{3,15},{4,8},{5,9},{6,10},{7,11},{8,4},{9,5},... | collective-permute-start | bytes 196616 | tf_op jit(solution)/shard_map/ppermute | solution.py:488
  81.7 5.6 %collective-permute-done.3.refs_2_ = bf16[32,1024]{1,0:T(8,128)(2,1)S(1)} collective-permute-done((bf16[32,1024]{1,0:T(8,128)(2,1)S(1)}, bf16[32,1024]{1,0:T(8,128)(2,1)S(1)}, u32[]{:S(2)}, u32[]{:S(2)}) %collective-permute-start.3) | collective-permute-done | bytes 65568 | tf_op jit(solution)/shard_map/ppermute | solution.py:488
  87.4 0.7 collective-permute-start.5
  88.1 1.5 %collective-permute-start.6 = (bf16[32,1024]{1,0:T(8,128)(2,1)S(1)}, bf16[32,1024]{1,0:T(8,128)(2,1)S(1)}, u32[]{:S(2)}, u32[]{:S(2)}) collective-permute-start(bf16[32,1024]{1,0:T(8,128)(2,1)S(1)} %sums.4.refs_0_), channel_id=1, source_target_pairs={{0,16},{1,17},{2,18},{3,19},{4,20},{5,21},{6,22},{7,23},{8,24},{9,... | collective-permute-start | bytes 196616 | tf_op jit(solution)/shard_map/ppermute | solution.py:488
  89.6 1.4 %collective-permute-start.7 = (bf16[32,1024]{1,0:T(8,128)(2,1)S(1)}, bf16[32,1024]{1,0:T(8,128)(2,1)S(1)}, u32[]{:S(2)}, u32[]{:S(2)}) collective-permute-start(bf16[32,1024]{1,0:T(8,128)(2,1)S(1)} %sums.4.refs_0_), channel_id=1, source_target_pairs={{0,18},{1,19},{2,16},{3,17},{4,22},{5,23},{6,20},{7,21},{8,26},{9,... | collective-permute-start | bytes 196616 | tf_op jit(solution)/shard_map/ppermute | solution.py:488
  91.0 1.1 %collective-permute-done.5.refs_1_ = bf16[32,1024]{1,0:T(8,128)(2,1)S(1)} collective-permute-done((bf16[32,1024]{1,0:T(8,128)(2,1)S(1)}, bf16[32,1024]{1,0:T(8,128)(2,1)S(1)}, u32[]{:S(2)}, u32[]{:S(2)}) %collective-permute-start.5) | collective-permute-done | bytes 65568 | tf_op jit(solution)/shard_map/ppermute | solution.py:488
  92.1 1.0 collective-permute-done.6.refs_2_
  93.0 1.8 %collective-permute-done.7.refs_3_ = bf16[32,1024]{1,0:T(8,128)(2,1)S(1)} collective-permute-done((bf16[32,1024]{1,0:T(8,128)(2,1)S(1)}, bf16[32,1024]{1,0:T(8,128)(2,1)S(1)}, u32[]{:S(2)}, u32[]{:S(2)}) %collective-permute-start.7) | collective-permute-done | bytes 65568 | tf_op jit(solution)/shard_map/ppermute | solution.py:488
  94.8 0.1 collective-permute-start.8
  94.9 1.3 %collective-permute-done.8.refs_3_ = bf16[2,32,1024]{2,1,0:T(8,128)(2,1)S(1)} collective-permute-done((bf16[2,32,1024]{2,1,0:T(8,128)(2,1)S(1)}, bf16[2,32,1024]{2,1,0:T(8,128)(2,1)S(1)}, u32[]{:S(2)}, u32[]{:S(2)}) %collective-permute-start.8) | collective-permute-done | bytes 131104 | tf_op jit(solution)/shard_map/ppermute | solution.py:488
  96.3 1.2 %table.1 = f32[256,1024]{1,0:T(8,128)} custom-call(s32[1,64]{1,0:T(1,128)S(1)} %copy-done.3, s32[1,64]{1,0:T(1,128)S(1)} %collective-permute-done.refs_1_, bf16[2,32,1024]{2,1,0:T(8,128)(2,1)S(1)} %sums.5.refs_2_, bf16[2,32,1024]{2,1,0:T(8,128)(2,1)S(1)} %collective-permute-done.8.refs_3_), custom_call_target="tpu_custom_call" | custom-call | tf_op jit(solution)/shard_map/table/pallas_call | solution.py:513
  (16 shorter events, 0.2 us)
Async XLA Ops:
  5.7 7.4 %copy-start.3 = (s32[1,64]{1,0:T(1,128)S(1)}, s32[1,64]{1,0:T(1,128)}, u32[]{:S(2)}) copy-start(s32[1,64]{1,0:T(1,128)} %refs_0_.1) | copy-start | bytes 772
  5.7 30.3 %all-to-all-start = ((bf16[16,32,1024]{2,1,0:T(8,128)(2,1)}), bf16[16,32,1024]{2,1,0:T(8,128)(2,1)S(1)}, u32[]{:S(2)}, u32[]{:S(2)}) async-start(bf16[16,32,1024]{2,1,0:T(8,128)(2,1)} %bitcast.20), calls=%async_computation | async-start | bytes 2097152 | tf_op jit(solution)/shard_map/all_to_all | solution.py:451
  13.1 5.3 %copy-start.4 = (bf16[1,128,4,1024]{3,2,1,0:T(4,128)(2,1)S(1)}, bf16[1,128,4,1024]{3,2,1,0:T(4,128)(2,1)}, u32[]{:S(2)}) copy-start(bf16[1,128,4,1024]{3,2,1,0:T(4,128)(2,1)} %param.7) | copy-start | bytes 3145732
  13.1 5.6 %collective-permute-start = (s32[1,64]{1,0:T(1,128)S(1)}, s32[1,64]{1,0:T(1,128)S(1)}, u32[]{:S(2)}, u32[]{:S(2)}) collective-permute-start(s32[1,64]{1,0:T(1,128)S(1)} %copy-done.3), channel_id=1, source_target_pairs={{0,16},{16,0},{1,17},{17,1},{2,18},{18,2},{3,19},{19,3},{4,20},{20... | collective-permute-start | bytes 776 | tf_op jit(solution)/shard_map/ppermute | solution.py:385
  18.7 17.3 %copy-start.2 = (f32[8,128]{1,0:T(8,128)S(1)}, f32[8,128]{1,0:T(8,128)}, u32[]{:S(2)}) copy-start(f32[8,128]{1,0:T(8,128)} %get-tuple-element.14.refs_0_) | copy-start | bytes 12292
  39.9 31.7 %copy-start = (bf16[8,64,1024]{2,1,0:T(8,128)(2,1)S(1)}, bf16[8,64,1024]{2,1,0:T(8,128)(2,1)}, u32[]{:S(2)}) copy-start(bf16[8,64,1024]{2,1,0:T(8,128)(2,1)} %get-tuple-element.11.embedded.other_embedded) | copy-start | bytes 3145732
  39.9 31.7 %copy-start.1 = (bf16[8,8,64,128]{3,2,1,0:T(8,128)(2,1)S(1)}, bf16[8,8,64,128]{3,2,1,0:T(8,128)(2,1)}, u32[]{:S(2)}) copy-start(bf16[8,8,64,128]{3,2,1,0:T(8,128)(2,1)} %get-tuple-element.12.weights.other_weights) | copy-start | bytes 3145732
  75.5 1.7 %collective-permute-start.1 = (bf16[32,1024]{1,0:T(8,128)(2,1)S(1)}, bf16[32,1024]{1,0:T(8,128)(2,1)S(1)}, u32[]{:S(2)}, u32[]{:S(2)}) collective-permute-start(bf16[32,1024]{1,0:T(8,128)(2,1)S(1)} %get-tuple-element.17), channel_id=1, source_target_pairs={{0,1},{1,0},{2,3},{3,2},{4,5},{5,4},{6,7},{7,6},{8,9},{9,8},{10,11... | collective-permute-start | bytes 196616 | tf_op jit(solution)/shard_map/ppermute | solution.py:488
  77.2 4.5 %collective-permute-start.2 = (bf16[32,1024]{1,0:T(8,128)(2,1)S(1)}, bf16[32,1024]{1,0:T(8,128)(2,1)S(1)}, u32[]{:S(2)}, u32[]{:S(2)}) collective-permute-start(bf16[32,1024]{1,0:T(8,128)(2,1)S(1)} %sums.3.refs_0_), channel_id=1, source_target_pairs={{0,4},{1,5},{2,6},{3,7},{4,0},{5,1},{6,2},{7,3},{8,12},{9,13},{10,... | collective-permute-start | bytes 196616 | tf_op jit(solution)/shard_map/ppermute | solution.py:488
  79.1 8.2 %collective-permute-start.3 = (bf16[32,1024]{1,0:T(8,128)(2,1)S(1)}, bf16[32,1024]{1,0:T(8,128)(2,1)S(1)}, u32[]{:S(2)}, u32[]{:S(2)}) collective-permute-start(bf16[32,1024]{1,0:T(8,128)(2,1)S(1)} %sums.3.refs_0_), channel_id=1, source_target_pairs={{0,8},{1,9},{2,10},{3,11},{4,12},{5,13},{6,14},{7,15},{8,0},{9,1},... | collective-permute-start | bytes 196616 | tf_op jit(solution)/shard_map/ppermute | solution.py:488
  80.0 7.3 %collective-permute-start.4 = (bf16[32,1024]{1,0:T(8,128)(2,1)S(1)}, bf16[32,1024]{1,0:T(8,128)(2,1)S(1)}, u32[]{:S(2)}, u32[]{:S(2)}) collective-permute-start(bf16[32,1024]{1,0:T(8,128)(2,1)S(1)} %sums.3.refs_0_), channel_id=1, source_target_pairs={{0,12},{1,13},{2,14},{3,15},{4,8},{5,9},{6,10},{7,11},{8,4},{9,5},... | collective-permute-start | bytes 196616 | tf_op jit(solution)/shard_map/ppermute | solution.py:488
  87.4 4.6 %collective-permute-start.5 = (bf16[32,1024]{1,0:T(8,128)(2,1)S(1)}, bf16[32,1024]{1,0:T(8,128)(2,1)S(1)}, u32[]{:S(2)}, u32[]{:S(2)}) collective-permute-start(bf16[32,1024]{1,0:T(8,128)(2,1)S(1)} %sums.4.refs_0_), channel_id=1, source_target_pairs={{0,2},{1,3},{2,0},{3,1},{4,6},{5,7},{6,4},{7,5},{8,10},{9,11},{10,... | collective-permute-start | bytes 196616 | tf_op jit(solution)/shard_map/ppermute | solution.py:488
  88.1 4.9 %collective-permute-start.6 = (bf16[32,1024]{1,0:T(8,128)(2,1)S(1)}, bf16[32,1024]{1,0:T(8,128)(2,1)S(1)}, u32[]{:S(2)}, u32[]{:S(2)}) collective-permute-start(bf16[32,1024]{1,0:T(8,128)(2,1)S(1)} %sums.4.refs_0_), channel_id=1, source_target_pairs={{0,16},{1,17},{2,18},{3,19},{4,20},{5,21},{6,22},{7,23},{8,24},{9,... | collective-permute-start | bytes 196616 | tf_op jit(solution)/shard_map/ppermute | solution.py:488
  89.6 5.2 %collective-permute-start.7 = (bf16[32,1024]{1,0:T(8,128)(2,1)S(1)}, bf16[32,1024]{1,0:T(8,128)(2,1)S(1)}, u32[]{:S(2)}, u32[]{:S(2)}) collective-permute-start(bf16[32,1024]{1,0:T(8,128)(2,1)S(1)} %sums.4.refs_0_), channel_id=1, source_target_pairs={{0,18},{1,19},{2,16},{3,17},{4,22},{5,23},{6,20},{7,21},{8,26},{9,... | collective-permute-start | bytes 196616 | tf_op jit(solution)/shard_map/ppermute | solution.py:488
  94.8 1.4 %collective-permute-start.8 = (bf16[2,32,1024]{2,1,0:T(8,128)(2,1)S(1)}, bf16[2,32,1024]{2,1,0:T(8,128)(2,1)S(1)}, u32[]{:S(2)}, u32[]{:S(2)}) collective-permute-start(bf16[2,32,1024]{2,1,0:T(8,128)(2,1)S(1)} %sums.5.refs_2_), channel_id=1, source_target_pairs={{0,1},{1,0},{2,3},{3,2},{4,5},{5,4},{6,7},{7,6},{8,9},{9,8},{10,11... | collective-permute-start | bytes 393224 | tf_op jit(solution)/shard_map/ppermute | solution.py:488

commit v5 on v4

--- a/solution.py
+++ b/solution.py
@@ -142,8 +142,33 @@
     return [items[start : start + size] for start in range(0, len(items), size)]
 
 
+def turned_stride(patches):
+    return patches + 1 if patches % SUBLANES == 0 else patches
+
+
+def turned_scratch(pairs, slots, patches):
+    return pltpu.VMEM((pairs, slots * turned_stride(patches), LANES), jnp.float32)
+
+
+def read_turned(ref, pair, slots, patches):
+    stride = turned_stride(patches)
+    if stride == patches:
+        return ref[pair]
+    pieces = [ref[pair, pl.ds(slot * stride, patches), :] for slot in range(slots)]
+    return jnp.concatenate(pieces, axis=0)
+
+
+def write_turned(ref, pair, rows, slots, patches):
+    stride = turned_stride(patches)
+    if stride == patches:
+        ref[pair] = rows
+        return
+    for slot in range(slots):
+        ref[pair, pl.ds(slot * stride, patches), :] = rows[slot * patches : (slot + 1) * patches]
+
+
 def of_patch(patch, slots, patches):
-    return pl.ds(patch, slots, stride=patches)
+    return pl.ds(patch, slots, stride=turned_stride(patches))
 
 
 def of_halves(halves, index):
@@ -192,7 +217,9 @@
         for (pair, p), value, result in zip(group, values, attended):
             by_electrode[pair, of_patch(p, slots, patches), :] = value.astype(jnp.float32) + result
     for pair in range(pairs):
-        mixed[:, pair_columns(pair)] = by_electrode[pair].astype(jnp.bfloat16)
+        mixed[:, pair_columns(pair)] = read_turned(by_electrode, pair, slots, patches).astype(
+            jnp.bfloat16
+        )
 
 
 def weights_kernel(width, counts, offsets, rows, tokens, embedded, weights, made, bias):
@@ -286,7 +313,8 @@
     ones = head_masks(width, 1.0)
     totals = [jnp.zeros((slots, LANES), jnp.float32) for _ in range(pairs)]
     for pair in range(pairs):
-        received[pair] = mixed_grad[:, step_columns(pair, model)].astype(jnp.float32)
+        arrived = mixed_grad[:, step_columns(pair, model)].astype(jnp.float32)
+        write_turned(received, pair, arrived, slots, patches)
     for group in in_groups(pairs, patches, SPATIAL_GROUP):
         cotangents = [
             received[pair, of_patch(p, slots, patches), :].astype(jnp.bfloat16)
@@ -394,7 +422,7 @@
     squares = pl.BlockSpec((local, pairs, slots, 2 * slots), lambda step: (0, step, 0, 0))
     flat_shape = jax.ShapeDtypeStruct((slots * local, model), jnp.bfloat16)
     plane_shape = jax.ShapeDtypeStruct(tokens.shape, jnp.bfloat16)
-    flat_scratch = pltpu.VMEM((pairs, slots * local, LANES), jnp.float32)
+    flat_scratch = turned_scratch(pairs, slots, local)
 
     strip = pl.BlockSpec((slots, STEP), lambda step: (0, step))
     pieces = model // PIECE

time: 97.8 us -> 97.7 us (level)
  no operation moved by 1% of the time
where the time goes in v5:
time: 97.7 us; the launch traced here: 97.4 us
  blocking collectives  31.6 us (32%)
  waiting for transfers between devices  29 us (30%)
  Pallas kernels  17.9 us (18%)
  starting transfers between devices  17.8 us (18%)
    all_to_all x1, blocking collectives, body(): lax.all_to_all(mixed_grad, 'shard', split_axis=0, concat_axis=0, tiled=True)  31.6 us
    all_to_all x1, waiting for transfers between devices, body(): lax.all_to_all(mixed, 'shard', split_axis=0, concat_axis=0, tiled=True)  17.3 us
    ppermute x8, waiting for transfers between devices, to_partner(): return lax.ppermute(array, ('group', 'shard'), pairs_of_devices)  11.7 us
    ppermute x8, starting transfers between devices, to_partner(): return lax.ppermute(array, ('group', 'shard'), pairs_of_devices)  8.84 us
    all_to_all x1, starting transfers between devices, body(): lax.all_to_all(mixed, 'shard', split_axis=0, concat_axis=0, tiled=True)  7.37 us
    pallas_call x1, Pallas kernels, body(): pl.pallas_call(functools.partial(spatial_kernel, width), grid=(steps,), o...  4.98 us
    pallas_call x1, Pallas kernels, body(): pl.pallas_call(functools.partial(spatial_back_kernel, width), grid=(steps...  3.98 us
    pallas_call x1, Pallas kernels, body(): pl.pallas_call(functools.partial(temporal_kernel, width, parts), out_shap...  3.86 us
  transfers between devices with their start and end apart: 10, of which 8 were waited for; matrix products, arithmetic and copies ran while one was open for 0% of the time, Pallas kernels for 4%

profile of v5, /device:TPU:0, one launch (start us, length us, event | category | flops | bytes accessed | tf_op | source)
XLA Modules:
  0.0 97.4 jit_solution(6349922628485961911)
XLA Ops:
  0.6 5.0 %spatial.1 = (bf16[64,1024]{1,0:T(8,128)(2,1)}, bf16[512,1024]{1,0:T(8,128)(2,1)}) custom-call(s32[1,2]{1,0:T(1,128)} %counts.3, s32[1,2]{1,0:T(1,128)} %offsets.3, s32[1,64]{1,0:T(1,128)} %refs_0_.1, bf16[512,1024]{1,0:T(8,128)(2,1)} %other_embedding.1, bf16[512,1024]{1,0:T(8,128)(2,1)} %other_embedding.1, bf16[8,64,1024]{2,1,0:T(8,128)(2,1)} %bitcast.16, ...), custom_call_target="tpu_custom_call" | custom-call | tf_op jit(solution)/shard_map/spatial/pallas_call | solution.py:445
  5.6 7.4 %all-to-all-start = ((bf16[16,32,1024]{2,1,0:T(8,128)(2,1)}), bf16[16,32,1024]{2,1,0:T(8,128)(2,1)S(1)}, u32[]{:S(2)}, u32[]{:S(2)}) async-start(bf16[16,32,1024]{2,1,0:T(8,128)(2,1)} %bitcast.20), calls=%async_computation | async-start | bytes 2097152 | tf_op jit(solution)/shard_map/all_to_all | solution.py:479
  13.0 1.6 %collective-permute-start = (s32[1,64]{1,0:T(1,128)S(1)}, s32[1,64]{1,0:T(1,128)S(1)}, u32[]{:S(2)}, u32[]{:S(2)}) collective-permute-start(s32[1,64]{1,0:T(1,128)S(1)} %copy-done.3), channel_id=1, source_target_pairs={{0,16},{16,0},{1,17},{17,1},{2,18},{18,2},{3,19},{19,3},{4,20},{20... | collective-permute-start | bytes 776 | tf_op jit(solution)/shard_map/ppermute | solution.py:413
  14.6 3.7 %weights.1 = (bf16[8,64,1024]{2,1,0:T(8,128)(2,1)}, bf16[8,8,64,128]{3,2,1,0:T(8,128)(2,1)}, f32[8,128]{1,0:T(8,128)}) custom-call(s32[1,2]{1,0:T(1,128)} %counts.3, s32[1,2]{1,0:T(1,128)} %offsets.3, bf16[64,1024]{1,0:T(8,128)(2,1)} %get-tuple-element.10.rows, bf16[8,64,1024]{2,1,0:T(8,128)(2,1)} %bitcast.18), custom_call_target="tpu_custom_call" | custom-call | flops 134217728 | bytes 3145728 | tf_op jit(solution)/shard_map/weights/pallas_call | solution.py:461
  18.3 0.3 copy.10
  18.7 17.3 %all-to-all-done = bf16[16,32,1024]{2,1,0:T(8,128)(2,1)S(1)} async-done(((bf16[16,32,1024]{2,1,0:T(8,128)(2,1)}), bf16[16,32,1024]{2,1,0:T(8,128)(2,1)S(1)}, u32[]{:S(2)}, u32[]{:S(2)}) %all-to-all-start) | async-done | bytes 1048608 | tf_op jit(solution)/shard_map/all_to_all | solution.py:479
  35.9 3.9 %temporal.1 = bf16[512,1024]{1,0:T(8,128)(2,1)S(1)} custom-call(bf16[512,1024]{1,0:T(8,128)(2,1)S(1)} %bitcast.13, bf16[4,128,1024]{2,1,0:T(8,128)(2,1)S(1)} %bitcast.14, f32[8,128]{1,0:T(8,128)S(1)} %copy-done.2, s32[1,64]{1,0:T(1,128)S(1)} %collective-permute-done.refs_1_), custom_call_target="tpu_custom_call" | custom-call | tf_op jit(solution)/shard_map/temporal/pallas_call | solution.py:480
  39.8 31.6 %all_to_all.22 = bf16[16,32,1024]{2,1,0:T(8,128)(2,1)S(1)} all-to-all(bf16[16,32,1024]{2,1,0:T(8,128)(2,1)S(1)} %bitcast.15), channel_id=1, replica_groups=mesh['group'=2,'shard'=16] {'shard'}, dimensions={0} | all-to-all | bytes 2097152 | tf_op jit(solution)/shard_map/all_to_all | solution.py:490
  71.5 4.0 %spatial_back.1 = (bf16[8,64,1024]{2,1,0:T(8,128)(2,1)}, bf16[32,1024]{1,0:T(8,128)(2,1)S(1)}, bf16[32,1024]{1,0:T(8,128)(2,1)S(1)}) custom-call(bf16[8,64,1024]{2,1,0:T(8,128)(2,1)S(1)} %copy-done, bf16[8,64,1024]{2,1,0:T(8,128)(2,1)S(1)} %copy-done, bf16[8,8,64,128]{3,2,1,0:T(8,128)(2,1)S(1)} %copy-done.1, bf16[8,8,64,128]{3,2,1,0:T(8,128)(2,1)S(1)} %copy-done.1, ...), custom_call_target="tpu_custom_call" | custom-call | tf_op jit(solution)/shard_map/spatial_back/pallas_call | solution.py:492
  75.5 0.8 collective-permute-start.1
  76.2 0.9 collective-permute-done.1.arrived
  77.1 1.9 %collective-permute-start.2 = (bf16[32,1024]{1,0:T(8,128)(2,1)S(1)}, bf16[32,1024]{1,0:T(8,128)(2,1)S(1)}, u32[]{:S(2)}, u32[]{:S(2)}) collective-permute-start(bf16[32,1024]{1,0:T(8,128)(2,1)S(1)} %sums.3.refs_0_), channel_id=1, source_target_pairs={{0,4},{1,5},{2,6},{3,7},{4,0},{5,1},{6,2},{7,3},{8,12},{9,13},{10,... | collective-permute-start | bytes 196616 | tf_op jit(solution)/shard_map/ppermute | solution.py:516
  79.1 0.9 collective-permute-start.3
  80.0 1.6 %collective-permute-start.4 = (bf16[32,1024]{1,0:T(8,128)(2,1)S(1)}, bf16[32,1024]{1,0:T(8,128)(2,1)S(1)}, u32[]{:S(2)}, u32[]{:S(2)}) collective-permute-start(bf16[32,1024]{1,0:T(8,128)(2,1)S(1)} %sums.3.refs_0_), channel_id=1, source_target_pairs={{0,12},{1,13},{2,14},{3,15},{4,8},{5,9},{6,10},{7,11},{8,4},{9,5},... | collective-permute-start | bytes 196616 | tf_op jit(solution)/shard_map/ppermute | solution.py:516
  81.6 0.1 collective-permute-done.2.refs_1_
  81.7 5.6 %collective-permute-done.3.refs_2_ = bf16[32,1024]{1,0:T(8,128)(2,1)S(1)} collective-permute-done((bf16[32,1024]{1,0:T(8,128)(2,1)S(1)}, bf16[32,1024]{1,0:T(8,128)(2,1)S(1)}, u32[]{:S(2)}, u32[]{:S(2)}) %collective-permute-start.3) | collective-permute-done | bytes 65568 | tf_op jit(solution)/shard_map/ppermute | solution.py:516
  87.4 0.7 collective-permute-start.5
  88.1 1.5 %collective-permute-start.6 = (bf16[32,1024]{1,0:T(8,128)(2,1)S(1)}, bf16[32,1024]{1,0:T(8,128)(2,1)S(1)}, u32[]{:S(2)}, u32[]{:S(2)}) collective-permute-start(bf16[32,1024]{1,0:T(8,128)(2,1)S(1)} %sums.4.refs_0_), channel_id=1, source_target_pairs={{0,16},{1,17},{2,18},{3,19},{4,20},{5,21},{6,22},{7,23},{8,24},{9,... | collective-permute-start | bytes 196616 | tf_op jit(solution)/shard_map/ppermute | solution.py:516
  89.6 1.4 %collective-permute-start.7 = (bf16[32,1024]{1,0:T(8,128)(2,1)S(1)}, bf16[32,1024]{1,0:T(8,128)(2,1)S(1)}, u32[]{:S(2)}, u32[]{:S(2)}) collective-permute-start(bf16[32,1024]{1,0:T(8,128)(2,1)S(1)} %sums.4.refs_0_), channel_id=1, source_target_pairs={{0,18},{1,19},{2,16},{3,17},{4,22},{5,23},{6,20},{7,21},{8,26},{9,... | collective-permute-start | bytes 196616 | tf_op jit(solution)/shard_map/ppermute | solution.py:516
  90.9 1.1 %collective-permute-done.5.refs_1_ = bf16[32,1024]{1,0:T(8,128)(2,1)S(1)} collective-permute-done((bf16[32,1024]{1,0:T(8,128)(2,1)S(1)}, bf16[32,1024]{1,0:T(8,128)(2,1)S(1)}, u32[]{:S(2)}, u32[]{:S(2)}) %collective-permute-start.5) | collective-permute-done | bytes 65568 | tf_op jit(solution)/shard_map/ppermute | solution.py:516
  92.0 1.0 collective-permute-done.6.refs_2_
  93.0 1.8 %collective-permute-done.7.refs_3_ = bf16[32,1024]{1,0:T(8,128)(2,1)S(1)} collective-permute-done((bf16[32,1024]{1,0:T(8,128)(2,1)S(1)}, bf16[32,1024]{1,0:T(8,128)(2,1)S(1)}, u32[]{:S(2)}, u32[]{:S(2)}) %collective-permute-start.7) | collective-permute-done | bytes 65568 | tf_op jit(solution)/shard_map/ppermute | solution.py:516
  94.9 1.3 %collective-permute-done.8.refs_3_ = bf16[2,32,1024]{2,1,0:T(8,128)(2,1)S(1)} collective-permute-done((bf16[2,32,1024]{2,1,0:T(8,128)(2,1)S(1)}, bf16[2,32,1024]{2,1,0:T(8,128)(2,1)S(1)}, u32[]{:S(2)}, u32[]{:S(2)}) %collective-permute-start.8) | collective-permute-done | bytes 131104 | tf_op jit(solution)/shard_map/ppermute | solution.py:516
  96.2 1.2 %table.1 = f32[256,1024]{1,0:T(8,128)} custom-call(s32[1,64]{1,0:T(1,128)S(1)} %copy-done.3, s32[1,64]{1,0:T(1,128)S(1)} %collective-permute-done.refs_1_, bf16[2,32,1024]{2,1,0:T(8,128)(2,1)S(1)} %sums.5.refs_2_, bf16[2,32,1024]{2,1,0:T(8,128)(2,1)S(1)} %collective-permute-done.8.refs_3_), custom_call_target="tpu_custom_call" | custom-call | tf_op jit(solution)/shard_map/table/pallas_call | solution.py:541
  (16 shorter events, 0.2 us)
Async XLA Ops:
  5.6 7.4 %copy-start.3 = (s32[1,64]{1,0:T(1,128)S(1)}, s32[1,64]{1,0:T(1,128)}, u32[]{:S(2)}) copy-start(s32[1,64]{1,0:T(1,128)} %refs_0_.1) | copy-start | bytes 772
  5.6 30.3 %all-to-all-start = ((bf16[16,32,1024]{2,1,0:T(8,128)(2,1)}), bf16[16,32,1024]{2,1,0:T(8,128)(2,1)S(1)}, u32[]{:S(2)}, u32[]{:S(2)}) async-start(bf16[16,32,1024]{2,1,0:T(8,128)(2,1)} %bitcast.20), calls=%async_computation | async-start | bytes 2097152 | tf_op jit(solution)/shard_map/all_to_all | solution.py:479
  13.0 5.3 %copy-start.4 = (bf16[1,128,4,1024]{3,2,1,0:T(4,128)(2,1)S(1)}, bf16[1,128,4,1024]{3,2,1,0:T(4,128)(2,1)}, u32[]{:S(2)}) copy-start(bf16[1,128,4,1024]{3,2,1,0:T(4,128)(2,1)} %param.7) | copy-start | bytes 3145732
  13.0 5.7 %collective-permute-start = (s32[1,64]{1,0:T(1,128)S(1)}, s32[1,64]{1,0:T(1,128)S(1)}, u32[]{:S(2)}, u32[]{:S(2)}) collective-permute-start(s32[1,64]{1,0:T(1,128)S(1)} %copy-done.3), channel_id=1, source_target_pairs={{0,16},{16,0},{1,17},{17,1},{2,18},{18,2},{3,19},{19,3},{4,20},{20... | collective-permute-start | bytes 776 | tf_op jit(solution)/shard_map/ppermute | solution.py:413
  18.7 17.3 %copy-start.2 = (f32[8,128]{1,0:T(8,128)S(1)}, f32[8,128]{1,0:T(8,128)}, u32[]{:S(2)}) copy-start(f32[8,128]{1,0:T(8,128)} %get-tuple-element.14.refs_0_) | copy-start | bytes 12292
  39.8 31.7 %copy-start = (bf16[8,64,1024]{2,1,0:T(8,128)(2,1)S(1)}, bf16[8,64,1024]{2,1,0:T(8,128)(2,1)}, u32[]{:S(2)}) copy-start(bf16[8,64,1024]{2,1,0:T(8,128)(2,1)} %get-tuple-element.11.embedded.other_embedded) | copy-start | bytes 3145732
  39.8 31.7 %copy-start.1 = (bf16[8,8,64,128]{3,2,1,0:T(8,128)(2,1)S(1)}, bf16[8,8,64,128]{3,2,1,0:T(8,128)(2,1)}, u32[]{:S(2)}) copy-start(bf16[8,8,64,128]{3,2,1,0:T(8,128)(2,1)} %get-tuple-element.12.weights.other_weights) | copy-start | bytes 3145732
  75.5 1.7 %collective-permute-start.1 = (bf16[32,1024]{1,0:T(8,128)(2,1)S(1)}, bf16[32,1024]{1,0:T(8,128)(2,1)S(1)}, u32[]{:S(2)}, u32[]{:S(2)}) collective-permute-start(bf16[32,1024]{1,0:T(8,128)(2,1)S(1)} %get-tuple-element.17), channel_id=1, source_target_pairs={{0,1},{1,0},{2,3},{3,2},{4,5},{5,4},{6,7},{7,6},{8,9},{9,8},{10,11... | collective-permute-start | bytes 196616 | tf_op jit(solution)/shard_map/ppermute | solution.py:516
  77.1 4.5 %collective-permute-start.2 = (bf16[32,1024]{1,0:T(8,128)(2,1)S(1)}, bf16[32,1024]{1,0:T(8,128)(2,1)S(1)}, u32[]{:S(2)}, u32[]{:S(2)}) collective-permute-start(bf16[32,1024]{1,0:T(8,128)(2,1)S(1)} %sums.3.refs_0_), channel_id=1, source_target_pairs={{0,4},{1,5},{2,6},{3,7},{4,0},{5,1},{6,2},{7,3},{8,12},{9,13},{10,... | collective-permute-start | bytes 196616 | tf_op jit(solution)/shard_map/ppermute | solution.py:516
  79.1 8.2 %collective-permute-start.3 = (bf16[32,1024]{1,0:T(8,128)(2,1)S(1)}, bf16[32,1024]{1,0:T(8,128)(2,1)S(1)}, u32[]{:S(2)}, u32[]{:S(2)}) collective-permute-start(bf16[32,1024]{1,0:T(8,128)(2,1)S(1)} %sums.3.refs_0_), channel_id=1, source_target_pairs={{0,8},{1,9},{2,10},{3,11},{4,12},{5,13},{6,14},{7,15},{8,0},{9,1},... | collective-permute-start | bytes 196616 | tf_op jit(solution)/shard_map/ppermute | solution.py:516
  80.0 7.3 %collective-permute-start.4 = (bf16[32,1024]{1,0:T(8,128)(2,1)S(1)}, bf16[32,1024]{1,0:T(8,128)(2,1)S(1)}, u32[]{:S(2)}, u32[]{:S(2)}) collective-permute-start(bf16[32,1024]{1,0:T(8,128)(2,1)S(1)} %sums.3.refs_0_), channel_id=1, source_target_pairs={{0,12},{1,13},{2,14},{3,15},{4,8},{5,9},{6,10},{7,11},{8,4},{9,5},... | collective-permute-start | bytes 196616 | tf_op jit(solution)/shard_map/ppermute | solution.py:516
  87.4 4.6 %collective-permute-start.5 = (bf16[32,1024]{1,0:T(8,128)(2,1)S(1)}, bf16[32,1024]{1,0:T(8,128)(2,1)S(1)}, u32[]{:S(2)}, u32[]{:S(2)}) collective-permute-start(bf16[32,1024]{1,0:T(8,128)(2,1)S(1)} %sums.4.refs_0_), channel_id=1, source_target_pairs={{0,2},{1,3},{2,0},{3,1},{4,6},{5,7},{6,4},{7,5},{8,10},{9,11},{10,... | collective-permute-start | bytes 196616 | tf_op jit(solution)/shard_map/ppermute | solution.py:516
  88.1 4.9 %collective-permute-start.6 = (bf16[32,1024]{1,0:T(8,128)(2,1)S(1)}, bf16[32,1024]{1,0:T(8,128)(2,1)S(1)}, u32[]{:S(2)}, u32[]{:S(2)}) collective-permute-start(bf16[32,1024]{1,0:T(8,128)(2,1)S(1)} %sums.4.refs_0_), channel_id=1, source_target_pairs={{0,16},{1,17},{2,18},{3,19},{4,20},{5,21},{6,22},{7,23},{8,24},{9,... | collective-permute-start | bytes 196616 | tf_op jit(solution)/shard_map/ppermute | solution.py:516
  89.6 5.2 %collective-permute-start.7 = (bf16[32,1024]{1,0:T(8,128)(2,1)S(1)}, bf16[32,1024]{1,0:T(8,128)(2,1)S(1)}, u32[]{:S(2)}, u32[]{:S(2)}) collective-permute-start(bf16[32,1024]{1,0:T(8,128)(2,1)S(1)} %sums.4.refs_0_), channel_id=1, source_target_pairs={{0,18},{1,19},{2,16},{3,17},{4,22},{5,23},{6,20},{7,21},{8,26},{9,... | collective-permute-start | bytes 196616 | tf_op jit(solution)/shard_map/ppermute | solution.py:516
  94.8 1.4 %collective-permute-start.8 = (bf16[2,32,1024]{2,1,0:T(8,128)(2,1)S(1)}, bf16[2,32,1024]{2,1,0:T(8,128)(2,1)S(1)}, u32[]{:S(2)}, u32[]{:S(2)}) collective-permute-start(bf16[2,32,1024]{2,1,0:T(8,128)(2,1)S(1)} %sums.5.refs_2_), channel_id=1, source_target_pairs={{0,1},{1,0},{2,3},{3,2},{4,5},{5,4},{6,7},{7,6},{8,9},{9,8},{10,11... | collective-permute-start | bytes 393224 | tf_op jit(solution)/shard_map/ppermute | solution.py:516

commit v6 on v5

--- a/solution.py
+++ b/solution.py
@@ -15,7 +15,7 @@
 SUBLANES = 8
 STEP = 512
 PIECES = 8
-PIECE = 256
+PIECE = 512
 PLANE = 4
 SPATIAL_GROUP = 32
 TEMPORAL_GROUP = 8

time: 97.7 us -> 97.7 us (level)
  no operation moved by 1% of the time
where the time goes in v6:
time: 97.7 us; the launch traced here: 97.4 us
  blocking collectives  31.6 us (32%)
  waiting for transfers between devices  29 us (30%)
  Pallas kernels  17.9 us (18%)
  starting transfers between devices  17.8 us (18%)
    all_to_all x1, blocking collectives, body(): lax.all_to_all(mixed_grad, 'shard', split_axis=0, concat_axis=0, tiled=True)  31.6 us
    all_to_all x1, waiting for transfers between devices, body(): lax.all_to_all(mixed, 'shard', split_axis=0, concat_axis=0, tiled=True)  17.3 us
    ppermute x8, waiting for transfers between devices, to_partner(): return lax.ppermute(array, ('group', 'shard'), pairs_of_devices)  11.7 us
    ppermute x8, starting transfers between devices, to_partner(): return lax.ppermute(array, ('group', 'shard'), pairs_of_devices)  8.84 us
    all_to_all x1, starting transfers between devices, body(): lax.all_to_all(mixed, 'shard', split_axis=0, concat_axis=0, tiled=True)  7.37 us
    pallas_call x1, Pallas kernels, body(): pl.pallas_call(functools.partial(spatial_kernel, width), grid=(steps,), o...  4.98 us
    pallas_call x1, Pallas kernels, body(): pl.pallas_call(functools.partial(spatial_back_kernel, width), grid=(steps...  3.98 us
    pallas_call x1, Pallas kernels, body(): pl.pallas_call(functools.partial(temporal_kernel, width, parts), out_shap...  3.85 us
  transfers between devices with their start and end apart: 10, of which 8 were waited for; matrix products, arithmetic and copies ran while one was open for 0% of the time, Pallas kernels for 4%

profile of v6, /device:TPU:0, one launch (start us, length us, event | category | flops | bytes accessed | tf_op | source)
XLA Modules:
  0.0 97.4 jit_solution(6924086035178082311)
XLA Ops:
  0.6 5.0 %spatial.1 = (bf16[64,1024]{1,0:T(8,128)(2,1)}, bf16[512,1024]{1,0:T(8,128)(2,1)}) custom-call(s32[1,2]{1,0:T(1,128)} %counts.3, s32[1,2]{1,0:T(1,128)} %offsets.3, s32[1,64]{1,0:T(1,128)} %refs_0_.1, bf16[512,1024]{1,0:T(8,128)(2,1)} %other_embedding.1, bf16[512,1024]{1,0:T(8,128)(2,1)} %other_embedding.1, bf16[8,64,1024]{2,1,0:T(8,128)(2,1)} %bitcast.16, ...), custom_call_target="tpu_custom_call" | custom-call | tf_op jit(solution)/shard_map/spatial/pallas_call | solution.py:445
  5.6 7.4 %all-to-all-start = ((bf16[16,32,1024]{2,1,0:T(8,128)(2,1)}), bf16[16,32,1024]{2,1,0:T(8,128)(2,1)S(1)}, u32[]{:S(2)}, u32[]{:S(2)}) async-start(bf16[16,32,1024]{2,1,0:T(8,128)(2,1)} %bitcast.20), calls=%async_computation | async-start | bytes 2097152 | tf_op jit(solution)/shard_map/all_to_all | solution.py:479
  13.0 1.6 %collective-permute-start = (s32[1,64]{1,0:T(1,128)S(1)}, s32[1,64]{1,0:T(1,128)S(1)}, u32[]{:S(2)}, u32[]{:S(2)}) collective-permute-start(s32[1,64]{1,0:T(1,128)S(1)} %copy-done.3), channel_id=1, source_target_pairs={{0,16},{16,0},{1,17},{17,1},{2,18},{18,2},{3,19},{19,3},{4,20},{20... | collective-permute-start | bytes 776 | tf_op jit(solution)/shard_map/ppermute | solution.py:413
  14.6 3.7 %weights.1 = (bf16[8,64,1024]{2,1,0:T(8,128)(2,1)}, bf16[8,8,64,128]{3,2,1,0:T(8,128)(2,1)}, f32[8,128]{1,0:T(8,128)}) custom-call(s32[1,2]{1,0:T(1,128)} %counts.3, s32[1,2]{1,0:T(1,128)} %offsets.3, bf16[64,1024]{1,0:T(8,128)(2,1)} %get-tuple-element.10.rows, bf16[8,64,1024]{2,1,0:T(8,128)(2,1)} %bitcast.18), custom_call_target="tpu_custom_call" | custom-call | flops 134217728 | bytes 3145728 | tf_op jit(solution)/shard_map/weights/pallas_call | solution.py:461
  18.3 0.3 copy.10
  18.7 17.3 %all-to-all-done = bf16[16,32,1024]{2,1,0:T(8,128)(2,1)S(1)} async-done(((bf16[16,32,1024]{2,1,0:T(8,128)(2,1)}), bf16[16,32,1024]{2,1,0:T(8,128)(2,1)S(1)}, u32[]{:S(2)}, u32[]{:S(2)}) %all-to-all-start) | async-done | bytes 1048608 | tf_op jit(solution)/shard_map/all_to_all | solution.py:479
  35.9 3.8 %temporal.1 = bf16[512,1024]{1,0:T(8,128)(2,1)S(1)} custom-call(bf16[512,1024]{1,0:T(8,128)(2,1)S(1)} %bitcast.13, bf16[4,128,1024]{2,1,0:T(8,128)(2,1)S(1)} %bitcast.14, f32[8,128]{1,0:T(8,128)S(1)} %copy-done.2, s32[1,64]{1,0:T(1,128)S(1)} %collective-permute-done.refs_1_), custom_call_target="tpu_custom_call" | custom-call | tf_op jit(solution)/shard_map/temporal/pallas_call | solution.py:480
  39.8 31.6 %all_to_all.22 = bf16[16,32,1024]{2,1,0:T(8,128)(2,1)S(1)} all-to-all(bf16[16,32,1024]{2,1,0:T(8,128)(2,1)S(1)} %bitcast.15), channel_id=1, replica_groups=mesh['group'=2,'shard'=16] {'shard'}, dimensions={0} | all-to-all | bytes 2097152 | tf_op jit(solution)/shard_map/all_to_all | solution.py:490
  71.5 4.0 %spatial_back.1 = (bf16[8,64,1024]{2,1,0:T(8,128)(2,1)}, bf16[32,1024]{1,0:T(8,128)(2,1)S(1)}, bf16[32,1024]{1,0:T(8,128)(2,1)S(1)}) custom-call(bf16[8,64,1024]{2,1,0:T(8,128)(2,1)S(1)} %copy-done, bf16[8,64,1024]{2,1,0:T(8,128)(2,1)S(1)} %copy-done, bf16[8,8,64,128]{3,2,1,0:T(8,128)(2,1)S(1)} %copy-done.1, bf16[8,8,64,128]{3,2,1,0:T(8,128)(2,1)S(1)} %copy-done.1, ...), custom_call_target="tpu_custom_call" | custom-call | tf_op jit(solution)/shard_map/spatial_back/pallas_call | solution.py:492
  75.4 0.8 collective-permute-start.1
  76.2 0.9 collective-permute-done.1.arrived
  77.1 1.9 %collective-permute-start.2 = (bf16[32,1024]{1,0:T(8,128)(2,1)S(1)}, bf16[32,1024]{1,0:T(8,128)(2,1)S(1)}, u32[]{:S(2)}, u32[]{:S(2)}) collective-permute-start(bf16[32,1024]{1,0:T(8,128)(2,1)S(1)} %sums.3.refs_0_), channel_id=1, source_target_pairs={{0,4},{1,5},{2,6},{3,7},{4,0},{5,1},{6,2},{7,3},{8,12},{9,13},{10,... | collective-permute-start | bytes 196616 | tf_op jit(solution)/shard_map/ppermute | solution.py:516
  79.1 0.9 collective-permute-start.3
  80.0 1.6 %collective-permute-start.4 = (bf16[32,1024]{1,0:T(8,128)(2,1)S(1)}, bf16[32,1024]{1,0:T(8,128)(2,1)S(1)}, u32[]{:S(2)}, u32[]{:S(2)}) collective-permute-start(bf16[32,1024]{1,0:T(8,128)(2,1)S(1)} %sums.3.refs_0_), channel_id=1, source_target_pairs={{0,12},{1,13},{2,14},{3,15},{4,8},{5,9},{6,10},{7,11},{8,4},{9,5},... | collective-permute-start | bytes 196616 | tf_op jit(solution)/shard_map/ppermute | solution.py:516
  81.6 0.1 collective-permute-done.2.refs_1_
  81.7 5.6 %collective-permute-done.3.refs_2_ = bf16[32,1024]{1,0:T(8,128)(2,1)S(1)} collective-permute-done((bf16[32,1024]{1,0:T(8,128)(2,1)S(1)}, bf16[32,1024]{1,0:T(8,128)(2,1)S(1)}, u32[]{:S(2)}, u32[]{:S(2)}) %collective-permute-start.3) | collective-permute-done | bytes 65568 | tf_op jit(solution)/shard_map/ppermute | solution.py:516
  87.4 0.7 collective-permute-start.5
  88.0 1.5 %collective-permute-start.6 = (bf16[32,1024]{1,0:T(8,128)(2,1)S(1)}, bf16[32,1024]{1,0:T(8,128)(2,1)S(1)}, u32[]{:S(2)}, u32[]{:S(2)}) collective-permute-start(bf16[32,1024]{1,0:T(8,128)(2,1)S(1)} %sums.4.refs_0_), channel_id=1, source_target_pairs={{0,16},{1,17},{2,18},{3,19},{4,20},{5,21},{6,22},{7,23},{8,24},{9,... | collective-permute-start | bytes 196616 | tf_op jit(solution)/shard_map/ppermute | solution.py:516
  89.6 1.4 %collective-permute-start.7 = (bf16[32,1024]{1,0:T(8,128)(2,1)S(1)}, bf16[32,1024]{1,0:T(8,128)(2,1)S(1)}, u32[]{:S(2)}, u32[]{:S(2)}) collective-permute-start(bf16[32,1024]{1,0:T(8,128)(2,1)S(1)} %sums.4.refs_0_), channel_id=1, source_target_pairs={{0,18},{1,19},{2,16},{3,17},{4,22},{5,23},{6,20},{7,21},{8,26},{9,... | collective-permute-start | bytes 196616 | tf_op jit(solution)/shard_map/ppermute | solution.py:516
  90.9 1.1 %collective-permute-done.5.refs_1_ = bf16[32,1024]{1,0:T(8,128)(2,1)S(1)} collective-permute-done((bf16[32,1024]{1,0:T(8,128)(2,1)S(1)}, bf16[32,1024]{1,0:T(8,128)(2,1)S(1)}, u32[]{:S(2)}, u32[]{:S(2)}) %collective-permute-start.5) | collective-permute-done | bytes 65568 | tf_op jit(solution)/shard_map/ppermute | solution.py:516
  92.0 1.0 collective-permute-done.6.refs_2_
  93.0 1.8 %collective-permute-done.7.refs_3_ = bf16[32,1024]{1,0:T(8,128)(2,1)S(1)} collective-permute-done((bf16[32,1024]{1,0:T(8,128)(2,1)S(1)}, bf16[32,1024]{1,0:T(8,128)(2,1)S(1)}, u32[]{:S(2)}, u32[]{:S(2)}) %collective-permute-start.7) | collective-permute-done | bytes 65568 | tf_op jit(solution)/shard_map/ppermute | solution.py:516
  94.8 1.3 %collective-permute-done.8.refs_3_ = bf16[2,32,1024]{2,1,0:T(8,128)(2,1)S(1)} collective-permute-done((bf16[2,32,1024]{2,1,0:T(8,128)(2,1)S(1)}, bf16[2,32,1024]{2,1,0:T(8,128)(2,1)S(1)}, u32[]{:S(2)}, u32[]{:S(2)}) %collective-permute-start.8) | collective-permute-done | bytes 131104 | tf_op jit(solution)/shard_map/ppermute | solution.py:516
  96.2 1.2 %table.1 = f32[256,1024]{1,0:T(8,128)} custom-call(s32[1,64]{1,0:T(1,128)S(1)} %copy-done.3, s32[1,64]{1,0:T(1,128)S(1)} %collective-permute-done.refs_1_, bf16[2,32,1024]{2,1,0:T(8,128)(2,1)S(1)} %sums.5.refs_2_, bf16[2,32,1024]{2,1,0:T(8,128)(2,1)S(1)} %collective-permute-done.8.refs_3_), custom_call_target="tpu_custom_call" | custom-call | tf_op jit(solution)/shard_map/table/pallas_call | solution.py:541
  (16 shorter events, 0.2 us)
Async XLA Ops:
  5.6 7.4 %copy-start.3 = (s32[1,64]{1,0:T(1,128)S(1)}, s32[1,64]{1,0:T(1,128)}, u32[]{:S(2)}) copy-start(s32[1,64]{1,0:T(1,128)} %refs_0_.1) | copy-start | bytes 772
  5.6 30.3 %all-to-all-start = ((bf16[16,32,1024]{2,1,0:T(8,128)(2,1)}), bf16[16,32,1024]{2,1,0:T(8,128)(2,1)S(1)}, u32[]{:S(2)}, u32[]{:S(2)}) async-start(bf16[16,32,1024]{2,1,0:T(8,128)(2,1)} %bitcast.20), calls=%async_computation | async-start | bytes 2097152 | tf_op jit(solution)/shard_map/all_to_all | solution.py:479
  13.0 5.3 %copy-start.4 = (bf16[1,128,4,1024]{3,2,1,0:T(4,128)(2,1)S(1)}, bf16[1,128,4,1024]{3,2,1,0:T(4,128)(2,1)}, u32[]{:S(2)}) copy-start(bf16[1,128,4,1024]{3,2,1,0:T(4,128)(2,1)} %param.7) | copy-start | bytes 3145732
  13.0 5.7 %collective-permute-start = (s32[1,64]{1,0:T(1,128)S(1)}, s32[1,64]{1,0:T(1,128)S(1)}, u32[]{:S(2)}, u32[]{:S(2)}) collective-permute-start(s32[1,64]{1,0:T(1,128)S(1)} %copy-done.3), channel_id=1, source_target_pairs={{0,16},{16,0},{1,17},{17,1},{2,18},{18,2},{3,19},{19,3},{4,20},{20... | collective-permute-start | bytes 776 | tf_op jit(solution)/shard_map/ppermute | solution.py:413
  18.7 17.3 %copy-start.2 = (f32[8,128]{1,0:T(8,128)S(1)}, f32[8,128]{1,0:T(8,128)}, u32[]{:S(2)}) copy-start(f32[8,128]{1,0:T(8,128)} %get-tuple-element.14.refs_0_) | copy-start | bytes 12292
  39.8 31.7 %copy-start = (bf16[8,64,1024]{2,1,0:T(8,128)(2,1)S(1)}, bf16[8,64,1024]{2,1,0:T(8,128)(2,1)}, u32[]{:S(2)}) copy-start(bf16[8,64,1024]{2,1,0:T(8,128)(2,1)} %get-tuple-element.11.embedded.other_embedded) | copy-start | bytes 3145732
  39.8 31.7 %copy-start.1 = (bf16[8,8,64,128]{3,2,1,0:T(8,128)(2,1)S(1)}, bf16[8,8,64,128]{3,2,1,0:T(8,128)(2,1)}, u32[]{:S(2)}) copy-start(bf16[8,8,64,128]{3,2,1,0:T(8,128)(2,1)} %get-tuple-element.12.weights.other_weights) | copy-start | bytes 3145732
  75.4 1.7 %collective-permute-start.1 = (bf16[32,1024]{1,0:T(8,128)(2,1)S(1)}, bf16[32,1024]{1,0:T(8,128)(2,1)S(1)}, u32[]{:S(2)}, u32[]{:S(2)}) collective-permute-start(bf16[32,1024]{1,0:T(8,128)(2,1)S(1)} %get-tuple-element.17), channel_id=1, source_target_pairs={{0,1},{1,0},{2,3},{3,2},{4,5},{5,4},{6,7},{7,6},{8,9},{9,8},{10,11... | collective-permute-start | bytes 196616 | tf_op jit(solution)/shard_map/ppermute | solution.py:516
  77.1 4.5 %collective-permute-start.2 = (bf16[32,1024]{1,0:T(8,128)(2,1)S(1)}, bf16[32,1024]{1,0:T(8,128)(2,1)S(1)}, u32[]{:S(2)}, u32[]{:S(2)}) collective-permute-start(bf16[32,1024]{1,0:T(8,128)(2,1)S(1)} %sums.3.refs_0_), channel_id=1, source_target_pairs={{0,4},{1,5},{2,6},{3,7},{4,0},{5,1},{6,2},{7,3},{8,12},{9,13},{10,... | collective-permute-start | bytes 196616 | tf_op jit(solution)/shard_map/ppermute | solution.py:516
  79.1 8.2 %collective-permute-start.3 = (bf16[32,1024]{1,0:T(8,128)(2,1)S(1)}, bf16[32,1024]{1,0:T(8,128)(2,1)S(1)}, u32[]{:S(2)}, u32[]{:S(2)}) collective-permute-start(bf16[32,1024]{1,0:T(8,128)(2,1)S(1)} %sums.3.refs_0_), channel_id=1, source_target_pairs={{0,8},{1,9},{2,10},{3,11},{4,12},{5,13},{6,14},{7,15},{8,0},{9,1},... | collective-permute-start | bytes 196616 | tf_op jit(solution)/shard_map/ppermute | solution.py:516
  80.0 7.3 %collective-permute-start.4 = (bf16[32,1024]{1,0:T(8,128)(2,1)S(1)}, bf16[32,1024]{1,0:T(8,128)(2,1)S(1)}, u32[]{:S(2)}, u32[]{:S(2)}) collective-permute-start(bf16[32,1024]{1,0:T(8,128)(2,1)S(1)} %sums.3.refs_0_), channel_id=1, source_target_pairs={{0,12},{1,13},{2,14},{3,15},{4,8},{5,9},{6,10},{7,11},{8,4},{9,5},... | collective-permute-start | bytes 196616 | tf_op jit(solution)/shard_map/ppermute | solution.py:516
  87.4 4.6 %collective-permute-start.5 = (bf16[32,1024]{1,0:T(8,128)(2,1)S(1)}, bf16[32,1024]{1,0:T(8,128)(2,1)S(1)}, u32[]{:S(2)}, u32[]{:S(2)}) collective-permute-start(bf16[32,1024]{1,0:T(8,128)(2,1)S(1)} %sums.4.refs_0_), channel_id=1, source_target_pairs={{0,2},{1,3},{2,0},{3,1},{4,6},{5,7},{6,4},{7,5},{8,10},{9,11},{10,... | collective-permute-start | bytes 196616 | tf_op jit(solution)/shard_map/ppermute | solution.py:516
  88.0 4.9 %collective-permute-start.6 = (bf16[32,1024]{1,0:T(8,128)(2,1)S(1)}, bf16[32,1024]{1,0:T(8,128)(2,1)S(1)}, u32[]{:S(2)}, u32[]{:S(2)}) collective-permute-start(bf16[32,1024]{1,0:T(8,128)(2,1)S(1)} %sums.4.refs_0_), channel_id=1, source_target_pairs={{0,16},{1,17},{2,18},{3,19},{4,20},{5,21},{6,22},{7,23},{8,24},{9,... | collective-permute-start | bytes 196616 | tf_op jit(solution)/shard_map/ppermute | solution.py:516
  89.6 5.2 %collective-permute-start.7 = (bf16[32,1024]{1,0:T(8,128)(2,1)S(1)}, bf16[32,1024]{1,0:T(8,128)(2,1)S(1)}, u32[]{:S(2)}, u32[]{:S(2)}) collective-permute-start(bf16[32,1024]{1,0:T(8,128)(2,1)S(1)} %sums.4.refs_0_), channel_id=1, source_target_pairs={{0,18},{1,19},{2,16},{3,17},{4,22},{5,23},{6,20},{7,21},{8,26},{9,... | collective-permute-start | bytes 196616 | tf_op jit(solution)/shard_map/ppermute | solution.py:516
  94.8 1.4 %collective-permute-start.8 = (bf16[2,32,1024]{2,1,0:T(8,128)(2,1)S(1)}, bf16[2,32,1024]{2,1,0:T(8,128)(2,1)S(1)}, u32[]{:S(2)}, u32[]{:S(2)}) collective-permute-start(bf16[2,32,1024]{2,1,0:T(8,128)(2,1)S(1)} %sums.5.refs_2_), channel_id=1, source_target_pairs={{0,1},{1,0},{2,3},{3,2},{4,5},{5,4},{6,7},{7,6},{8,9},{9,8},{10,11... | collective-permute-start | bytes 393224 | tf_op jit(solution)/shard_map/ppermute | solution.py:516
